TPU v7x, 128 devices: a whole 4x4x4 slice. The times are simulated.
128 devices in a mesh: seq: 16 (over x_hi, y, core), tp: 8 (over z, x_lo).
Axes of the slice: x: 4 (x_hi: 2, x_lo: 2; x = x_hi * 2 + x_lo), y: 4, z: 4, core: 2. Of those that a mesh axis runs over, the one named last changes fastest.
Arguments:
- tokens: bfloat16 [4096, 2048], P('seq'), may hold values from -6 to 6
- gain_attn: float32 [2048], replicated, may hold values from 0.5 to 1.5
- w_query: bfloat16 [2048, 2048], P(None, 'tp'), may hold values from -0.125 to 0.125
- w_key: bfloat16 [2048, 2048], P(None, 'tp'), may hold values from -0.125 to 0.125
- w_value: bfloat16 [2048, 2048], P(None, 'tp'), may hold values from -0.125 to 0.125
- w_out: bfloat16 [2048, 2048], P('tp'), may hold values from -1.5 to 1.5
- gain_ffn: float32 [2048], replicated, may hold values from 0.5 to 1.5
- w_gate: bfloat16 [2048, 5504], P(None, 'tp'), may hold values from -0.125 to 0.125
- w_up: bfloat16 [2048, 5504], P(None, 'tp'), may hold values from -0.125 to 0.125
- w_down: bfloat16 [5504, 2048], P('tp'), may hold values from -0.078125 to 0.078125
- cotangent: bfloat16 [4096, 2048], P('seq'), may hold values from -6 to 6
Outputs:
- block_out: bfloat16 [4096, 2048], P('seq')
- grad_tokens: float32 [4096, 2048], P('seq')
- grad_gain_attn: float32 [2048], P('tp')
- grad_w_query: float32 [2048, 2048], P(None, 'tp')
- grad_w_key: float32 [2048, 2048], P(None, 'tp')
- grad_w_value: float32 [2048, 2048], P(None, 'tp')
- grad_w_out: float32 [2048, 2048], P('tp')
- grad_gain_ffn: float32 [2048], P('tp')
- grad_w_gate: float32 [2048, 5504], P(None, 'tp')
- grad_w_up: float32 [2048, 5504], P(None, 'tp')
- grad_w_down: float32 [5504, 2048], P('tp')
All inputs are finite; a program needn't handle non-finite values.
Results may differ from a plain program's by a relative error of at most 0.023.
Values may be sent and summed in bfloat16 or wider, within the bound.
No kernel may reach another device: no remote copies, remote signals or barrier semaphores. Data moves between devices by JAX's collectives and lax.ppermute only.
A program may use at most 192 MiB of HBM per device.

v0:
```python
import jax
import jax.numpy as jnp
from jax import lax
from jax.sharding import PartitionSpec as P

HD = 128
W = 1024


epsilon = 1e-06
masked_value = -1e30


def shifted(value, axis, steps):
    count = lax.axis_size(axis)
    first, last = (max(0, -steps), min(count, count - steps))
    return lax.ppermute(value, axis, [(source, source + steps) for source in range(first, last)])


def rms_factor(field_rows):
    return lax.rsqrt(jnp.mean(field_rows * field_rows, axis=-1, keepdims=True) + epsilon)


def norm_back(grad_normed, unit_rows, factor, gain_vec):
    scaled = grad_normed * gain_vec
    return factor * (scaled - unit_rows * jnp.mean(scaled * unit_rows, axis=-1, keepdims=True))


def matmul(left_matrix, right_matrix):
    return jnp.dot(left_matrix, right_matrix, preferred_element_type=jnp.float32)


def outer_sum(left_matrix, right_matrix):
    return lax.dot_general(
        left_matrix, right_matrix, (((0,), (0,)), ((), ())), preferred_element_type=jnp.float32
    )


def times_trans(left_matrix, right_matrix):
    return lax.dot_general(
        left_matrix, right_matrix, (((1,), (1,)), ((), ())), preferred_element_type=jnp.float32
    )


def window_mask(tok_rows, seq_index):
    offset = seq_index * tok_rows
    query_pos = offset + jnp.arange(tok_rows, dtype=jnp.int32)
    key_pos = offset - W + jnp.arange(W + tok_rows, dtype=jnp.int32)
    return (
        (key_pos[None, :] >= 0)
        & (key_pos[None, :] <= query_pos[:, None])
        & (key_pos[None, :] > query_pos[:, None] - W)
    )


def gather_window(key_rows, value_rows, reach_back):
    key_pieces = []
    value_pieces = []
    for distance in range(reach_back, 0, -1):
        arrived = shifted((key_rows, value_rows), "seq", distance)
        key_pieces.append(arrived[0])
        value_pieces.append(arrived[1])
    key_pieces.append(key_rows)
    value_pieces.append(value_rows)
    return (jnp.concatenate(key_pieces, axis=0), jnp.concatenate(value_pieces, axis=0))


def return_window(grad_key_all, grad_value_all, tok_rows, reach_back):
    own_keys = grad_key_all[reach_back * tok_rows :]
    own_values = grad_value_all[reach_back * tok_rows :]
    for distance in range(1, reach_back + 1):
        lower = (reach_back - distance) * tok_rows
        arrived = (
            shifted(
                grad_key_all[lower : lower + tok_rows].astype(jnp.bfloat16), "seq", -distance
            ).astype(jnp.float32),
            shifted(
                grad_value_all[lower : lower + tok_rows].astype(jnp.bfloat16), "seq", -distance
            ).astype(jnp.float32),
        )
        own_keys = own_keys + arrived[0]
        own_values = own_values + arrived[1]
    return (own_keys, own_values)


def head_scores(queries, key_all, allowed, score_scale):
    scores = (
        jnp.einsum("ihd,chd->hic", queries, key_all, preferred_element_type=jnp.float32)
        * score_scale
    )
    return jnp.where(allowed[None], scores, masked_value)


def on_device(
    tokens, gain_attn, w_query, w_key, w_value, w_out, gain_ffn, w_gate, w_up, w_down, cotangent
):
    tok_rows = tokens.shape[0]
    model_width = tokens.shape[1]
    local_heads = w_query.shape[1] // HD
    reach_back = W // tok_rows
    score_scale = HD ** (-0.5)
    allowed = window_mask(tok_rows, lax.axis_index("seq"))
    gain_share = model_width // lax.axis_size("tp")
    share_start = lax.axis_index("tp") * gain_share
    inputs = tokens.astype(jnp.float32)
    factor_attn = rms_factor(inputs)
    unit_attn = inputs * factor_attn
    normed_attn = (unit_attn * gain_attn).astype(jnp.bfloat16)
    query_rows = matmul(normed_attn, w_query).astype(jnp.bfloat16)
    key_rows = matmul(normed_attn, w_key).astype(jnp.bfloat16)
    value_rows = matmul(normed_attn, w_value).astype(jnp.bfloat16)
    key_window, value_window = gather_window(key_rows, value_rows, reach_back)
    queries = query_rows.reshape(tok_rows, local_heads, HD)
    key_all = key_window.reshape(-1, local_heads, HD)
    value_all = value_window.reshape(-1, local_heads, HD)
    scores = head_scores(queries, key_all, allowed, score_scale)
    row_peak = jnp.max(scores, axis=-1, keepdims=True)
    log_total = row_peak + jnp.log(jnp.sum(jnp.exp(scores - row_peak), axis=-1, keepdims=True))
    weights_low = jnp.exp(scores - log_total).astype(jnp.bfloat16)
    mixed_heads = jnp.einsum(
        "hic,chd->ihd", weights_low, value_all, preferred_element_type=jnp.float32
    )
    heads_out = mixed_heads.reshape(tok_rows, -1).astype(jnp.bfloat16)
    hidden = inputs + lax.psum(matmul(heads_out, w_out), "tp")
    factor_ffn = rms_factor(hidden)
    unit_ffn = hidden * factor_ffn
    normed_rows = (unit_ffn * gain_ffn).astype(jnp.bfloat16)
    gate_pre = matmul(normed_rows, w_gate)
    up_pre = matmul(normed_rows, w_up)
    gate_sigmoid = jax.nn.sigmoid(gate_pre)
    gate_silu = gate_pre * gate_sigmoid
    activated = (gate_silu * up_pre).astype(jnp.bfloat16)
    ffn_total = lax.psum(matmul(activated, w_down).astype(jnp.bfloat16), "tp").astype(jnp.float32)
    out_rows = hidden + ffn_total
    grad_w_down = outer_sum(activated, cotangent)
    grad_act = times_trans(cotangent, w_down)
    grad_gate_pre = (
        grad_act * up_pre * gate_sigmoid * (1.0 + gate_pre * (1.0 - gate_sigmoid))
    ).astype(jnp.bfloat16)
    grad_up_pre = (grad_act * gate_silu).astype(jnp.bfloat16)
    grad_w_gate = outer_sum(normed_rows, grad_gate_pre)
    grad_w_up = outer_sum(normed_rows, grad_up_pre)
    grad_normed_ffn = lax.psum(
        times_trans(grad_gate_pre, w_gate) + times_trans(grad_up_pre, w_up), "tp"
    )
    gain_part = jnp.sum(grad_normed_ffn * unit_ffn, axis=0)
    grad_hidden = cotangent.astype(jnp.float32) + norm_back(
        grad_normed_ffn, unit_ffn, factor_ffn, gain_ffn
    )
    block_out = out_rows.astype(jnp.bfloat16)
    grad_gain_ffn = lax.dynamic_slice_in_dim(gain_part, share_start, gain_share)
    grad_hidden_low = grad_hidden.astype(jnp.bfloat16)
    grad_w_out = outer_sum(heads_out, grad_hidden_low)
    grad_heads = (
        times_trans(grad_hidden_low, w_out).astype(jnp.bfloat16).reshape(tok_rows, local_heads, HD)
    )
    key_window, value_window = gather_window(key_rows, value_rows, reach_back)
    key_all = key_window.reshape(-1, local_heads, HD)
    value_all = value_window.reshape(-1, local_heads, HD)
    scores = head_scores(queries, key_all, allowed, score_scale)
    weights_full = jnp.exp(scores - log_total)
    weights_low = weights_full.astype(jnp.bfloat16)
    grad_value_all = jnp.einsum(
        "hic,ihd->chd", weights_low, grad_heads, preferred_element_type=jnp.float32
    )
    grad_probs = jnp.einsum(
        "ihd,chd->hic", grad_heads, value_all, preferred_element_type=jnp.float32
    )
    row_inner = jnp.sum(weights_full * grad_probs, axis=-1, keepdims=True)
    grad_scores = (weights_full * (grad_probs - row_inner)).astype(jnp.bfloat16)
    grad_queries = (
        jnp.einsum("hic,chd->ihd", grad_scores, key_all, preferred_element_type=jnp.float32)
        * score_scale
    )
    grad_key_all = (
        jnp.einsum("hic,ihd->chd", grad_scores, queries, preferred_element_type=jnp.float32)
        * score_scale
    )
    own_keys, own_values = return_window(
        grad_key_all.reshape(key_all.shape[0], -1),
        grad_value_all.reshape(value_all.shape[0], -1),
        tok_rows,
        reach_back,
    )
    grad_query_low = grad_queries.reshape(tok_rows, -1).astype(jnp.bfloat16)
    grad_key_low = own_keys.astype(jnp.bfloat16)
    grad_value_low = own_values.astype(jnp.bfloat16)
    grad_w_query = outer_sum(normed_attn, grad_query_low)
    grad_w_key = outer_sum(normed_attn, grad_key_low)
    grad_w_value = outer_sum(normed_attn, grad_value_low)
    local_back = (
        times_trans(grad_query_low, w_query)
        + times_trans(grad_key_low, w_key)
        + times_trans(grad_value_low, w_value)
    )
    grad_normed_attn = lax.psum(local_back.astype(jnp.bfloat16), "tp").astype(jnp.float32)
    grad_gain_attn = lax.dynamic_slice_in_dim(
        jnp.sum(grad_normed_attn * unit_attn, axis=0), share_start, gain_share
    )
    grad_tokens = grad_hidden + norm_back(grad_normed_attn, unit_attn, factor_attn, gain_attn)
    summed = (
        lax.psum(grad_gain_attn.astype(jnp.bfloat16), "seq").astype(jnp.float32),
        lax.psum(grad_w_query.astype(jnp.bfloat16), "seq").astype(jnp.float32),
        lax.psum(grad_w_key.astype(jnp.bfloat16), "seq").astype(jnp.float32),
        lax.psum(grad_w_value.astype(jnp.bfloat16), "seq").astype(jnp.float32),
        lax.psum(grad_w_out.astype(jnp.bfloat16), "seq").astype(jnp.float32),
        lax.psum(grad_gain_ffn.astype(jnp.bfloat16), "seq").astype(jnp.float32),
        lax.psum(grad_w_gate.astype(jnp.bfloat16), "seq").astype(jnp.float32),
        lax.psum(grad_w_up.astype(jnp.bfloat16), "seq").astype(jnp.float32),
        lax.psum(grad_w_down.astype(jnp.bfloat16), "seq").astype(jnp.float32),
    )
    (
        grad_gain_attn,
        grad_w_query,
        grad_w_key,
        grad_w_value,
        grad_w_out,
        grad_gain_ffn,
        grad_w_gate,
        grad_w_up,
        grad_w_down,
    ) = summed
    return (
        block_out,
        grad_tokens,
        grad_gain_attn,
        grad_w_query,
        grad_w_key,
        grad_w_value,
        grad_w_out,
        grad_gain_ffn,
        grad_w_gate,
        grad_w_up,
        grad_w_down,
    )


def solution(mesh):
    return jax.shard_map(
        on_device,
        mesh=mesh,
        in_specs=(
            P("seq", None),
            P(),
            P(None, "tp"),
            P(None, "tp"),
            P(None, "tp"),
            P("tp", None),
            P(),
            P(None, "tp"),
            P(None, "tp"),
            P("tp", None),
            P("seq", None),
        ),
        out_specs=(
            P("seq", None),
            P("seq", None),
            P("tp"),
            P(None, "tp"),
            P(None, "tp"),
            P(None, "tp"),
            P("tp", None),
            P("tp"),
            P(None, "tp"),
            P(None, "tp"),
            P("tp", None),
        ),
        check_vma=False,
    )
```

profile of v0, /device:TPU:1, one launch (start us, length us, event | category | flops | bytes accessed | tf_op | source)
XLA Modules:
  0.0 647.3 jit_solution(13053191680176052331)
XLA Ops:
  8.9 2.8 convolution_convert_fusion.12
  11.7 4.6 collective-permute-start.3
  16.3 3.9 collective-permute-start.2
  20.2 2.9 collective-permute-start.1
  23.6 5.6 collective-permute-start.5
  29.2 3.3 collective-permute-start.4
  33.7 2.9 convolution_convert_fusion.11
  38.5 5.1 collective-permute-start.7
  43.6 6.4 collective-permute-start
  50.1 2.8 collective-permute-done
  67.4 110.1 %all-reduce.8.cloned.1.call-done = f32[256,2048]{1,0:T(8,128)} async-done(((f32[256,2048]{1,0:T(8,128)}), f32[256,2048]{1,0:T(8,128)}) %all-reduce.8.cloned.1.call-update) | async-done | bytes 2097168 | tf_op jit(solution)/shard_map/psum | solution.py:124
  191.2 3.0 convolution_convert_fusion.7
  194.1 100.9 %all-reduce.10.cloned.1.call-done = f32[256,2048]{1,0:T(8,128)} async-done(((f32[256,2048]{1,0:T(8,128)}), f32[256,2048]{1,0:T(8,128)}) %all-reduce.10.cloned.1.call-update) | async-done | bytes 2097168 | tf_op jit(solution)/shard_map/psum | solution.py:143
  295.1 2.9 multiply_reduce_fusion.1
  309.7 2.8 collective-permute-start.8
  317.9 3.2 collective-permute-start.12
  349.8 92.9 %all-reduce.14.cloned.1.call-done = (bf16[256,2048]{1,0:T(8,128)(2,1)}, bf16[256,2048]{1,0:T(8,128)(2,1)}) async-done(((bf16[256,2048]{1,0:T(8,128)(2,1)}, bf16[256,2048]{1,0:T(8,128)(2,1)}), (bf16[256,2048]{1,0:T(8,128)(2,1)}, bf16[256,2048]{1,0:T(8,128)(2,1)})) %all-reduce.14.cloned.1.call-update) | async-done | bytes 2097168 | tf_op jit(solution)/shard_map/psum | solution.py:133
  445.2 33.5 %all-reduce = (bf16[256]{0:T(256)(128)(2,1)S(1)}, bf16[256]{0:T(256)(128)(2,1)S(1)}) all-reduce(bf16[256]{0:T(256)(128)(2,1)S(1)} %dynamic_slice.11, bf16[256]{0:T(256)(128)(2,1)S(1)} %dynamic_slice.10), channel_id=1, replica_groups=mesh['seq'=16,'tp'=8] {'seq'}, use_global_device_ids=true, to_apply=%region_12.13 | all-reduce | flops 512 | bytes 2048 | tf_op jit(solution)/shard_map/psum | solution.py:202
  479.9 2.7 add_convert_fusion
  484.5 138.1 %all-reduce.12.cloned.1.call-done = (bf16[2048,256]{1,0:T(8,128)(2,1)}, bf16[2048,256]{1,0:T(8,128)(2,1)}, bf16[2048,256]{1,0:T(8,128)(2,1)}, bf16[256,2048]{1,0...) async-done(((bf16[2048,256]{1,0:T(8,128)(2,1)}, bf16[2048,256]{1,0:T(8,128)(2,1)}, bf16[2048,256]{1,0:T(8,128)(2,1)}, ...) | async-done | bytes 12648464 | tf_op jit(solution)/shard_map/psum | solution.py:203
  622.6 2.8 convert_element_type.238
  631.0 3.2 convert_element_type.248
  634.3 3.2 convert_element_type.250
  637.5 3.2 convert_element_type.252
  (187 shorter events, 90.0 us)
Async XLA Ops:
  7.2 178.2 %copy-start = (bf16[688,2048]{1,0:T(8,128)(2,1)S(1)}, bf16[688,2048]{1,0:T(8,128)(2,1)}, u32[]{:S(2)}) copy-start(bf16[688,2048]{1,0:T(8,128)(2,1)} %param.20) | copy-start | bytes 8454148
  7.2 170.3 %all-reduce.8.cloned.1.call-start = ((), (), s32[]{:S(2)}) async-start(), calls=%async_computation | async-start | bytes 4194304 | tf_op jit(solution)/shard_map/psum | solution.py:124
  11.7 45.4 %collective-permute-start.3 = (bf16[256,256]{1,0:T(8,128)(2,1)}, bf16[256,256]{1,0:T(8,128)(2,1)}, u32[]{:S(2)}, u32[]{:S(2)}) collective-permute-start(bf16[256,256]{1,0:T(8,128)(2,1)} %convolution_convert_fusion.12), channel_id=1, source_target_pairs={{0,8},{8,16},{16,24},{24,32},{32,40},{40,48},{48,56},{56,64},{64,7... | collective-permute-start | bytes 393224 | tf_op jit(solution)/shard_map/ppermute | solution.py:17
  16.3 39.2 %collective-permute-start.2 = (bf16[256,256]{1,0:T(8,128)(2,1)}, bf16[256,256]{1,0:T(8,128)(2,1)}, u32[]{:S(2)}, u32[]{:S(2)}) collective-permute-start(bf16[256,256]{1,0:T(8,128)(2,1)} %convolution_convert_fusion.12), channel_id=1, source_target_pairs={{0,16},{8,24},{16,32},{24,40},{32,48},{40,56},{48,64},{56,72},{64,... | collective-permute-start | bytes 393224 | tf_op jit(solution)/shard_map/ppermute | solution.py:17
  20.2 33.4 %collective-permute-start.1 = (bf16[256,256]{1,0:T(8,128)(2,1)}, bf16[256,256]{1,0:T(8,128)(2,1)S(1)}, u32[]{:S(2)}, u32[]{:S(2)}) collective-permute-start(bf16[256,256]{1,0:T(8,128)(2,1)} %convolution_convert_fusion.12), channel_id=1, source_target_pairs={{0,24},{8,32},{16,40},{24,48},{32,56},{40,64},{48,72},{56,80},{64,... | collective-permute-start | bytes 393224 | tf_op jit(solution)/shard_map/ppermute | solution.py:17
  23.6 14.9 %collective-permute-start.5 = (bf16[256,256]{1,0:T(8,128)(2,1)S(1)}, bf16[256,256]{1,0:T(8,128)(2,1)S(1)}, u32[]{:S(2)}, u32[]{:S(2)}) collective-permute-start(bf16[256,256]{1,0:T(8,128)(2,1)S(1)} %convolution_convert_fusion.10), channel_id=1, source_target_pairs={{0,24},{8,32},{16,40},{24,48},{32,56},{40,64},{48,72},{56,80},{64,... | collective-permute-start | bytes 393224 | tf_op jit(solution)/shard_map/ppermute | solution.py:17
  29.2 7.4 %collective-permute-start.4 = (bf16[256,256]{1,0:T(8,128)(2,1)S(1)}, bf16[256,256]{1,0:T(8,128)(2,1)S(1)}, u32[]{:S(2)}, u32[]{:S(2)}) collective-permute-start(bf16[256,256]{1,0:T(8,128)(2,1)S(1)} %convolution_convert_fusion.10), channel_id=1, source_target_pairs={{0,32},{8,40},{16,48},{24,56},{32,64},{40,72},{48,80},{56,88},{64,... | collective-permute-start | bytes 393224 | tf_op jit(solution)/shard_map/ppermute | solution.py:17
  36.6 7.0 %collective-permute-start.6 = (bf16[256,256]{1,0:T(8,128)(2,1)S(1)}, bf16[256,256]{1,0:T(8,128)(2,1)S(1)}, u32[]{:S(2)}, u32[]{:S(2)}) collective-permute-start(bf16[256,256]{1,0:T(8,128)(2,1)S(1)} %convolution_convert_fusion.10), channel_id=1, source_target_pairs={{0,16},{8,24},{16,32},{24,40},{32,48},{40,56},{48,64},{56,72},{64,... | collective-permute-start | bytes 393224 | tf_op jit(solution)/shard_map/ppermute | solution.py:17
  38.5 11.5 %collective-permute-start.7 = (bf16[256,256]{1,0:T(8,128)(2,1)S(1)}, bf16[256,256]{1,0:T(8,128)(2,1)S(1)}, u32[]{:S(2)}, u32[]{:S(2)}) collective-permute-start(bf16[256,256]{1,0:T(8,128)(2,1)S(1)} %convolution_convert_fusion.10), channel_id=1, source_target_pairs={{0,8},{8,16},{16,24},{24,32},{32,40},{40,48},{48,56},{56,64},{64,7... | collective-permute-start | bytes 393224 | tf_op jit(solution)/shard_map/ppermute | solution.py:17
  43.6 9.3 %collective-permute-start = (bf16[256,256]{1,0:T(8,128)(2,1)}, bf16[256,256]{1,0:T(8,128)(2,1)S(1)}, u32[]{:S(2)}, u32[]{:S(2)}) collective-permute-start(bf16[256,256]{1,0:T(8,128)(2,1)} %convolution_convert_fusion.12), channel_id=1, source_target_pairs={{0,32},{8,40},{16,48},{24,56},{32,64},{40,72},{48,80},{56,88},{64,... | collective-permute-start | bytes 393224 | tf_op jit(solution)/shard_map/ppermute | solution.py:17
  67.3 112.5 %copy-start.44 = (f32[2048]{0:T(1024)S(1)}, f32[2048]{0:T(1024)}, u32[]{:S(2)}) copy-start(f32[2048]{0:T(1024)} %param.17) | copy-start | bytes 24580
  67.3 227.8 %all-reduce.10.cloned.1.call-start = ((), (), s32[]{:S(2)}) async-start(), calls=%async_computation.1 | async-start | bytes 4194304 | tf_op jit(solution)/shard_map/psum | solution.py:143
  191.0 251.8 %all-reduce.14.cloned.1.call-start = ((), (), s32[]{:S(2)}) async-start(), calls=%async_computation.3 | async-start | bytes 4194304 | tf_op jit(solution)/shard_map/psum | solution.py:133
  194.1 103.9 %copy-start.5 = (f32[256,2048]{1,0:T(8,128)S(1)}, f32[256,2048]{1,0:T(8,128)}, u32[]{:S(2)}) copy-start(f32[256,2048]{1,0:T(8,128)} %copy-done.4) | copy-start | bytes 6291460
  307.1 21.7 %collective-permute-start.15 = (bf16[256,256]{0,1:T(8,128)(2,1)S(1)}, bf16[256,256]{0,1:T(8,128)(2,1)S(1)}, u32[]{:S(2)}, u32[]{:S(2)}) collective-permute-start(bf16[256,256]{0,1:T(8,128)(2,1)S(1)} %bitcast.110), channel_id=1, source_target_pairs={{32,0},{40,8},{48,16},{56,24},{64,32},{72,40},{80,48},{88,56},{96,... | collective-permute-start | bytes 393224 | tf_op jit(solution)/shard_map/ppermute | solution.py:17
  308.4 9.5 %collective-permute-start.11 = (bf16[256,256]{0,1:T(8,128)(2,1)S(1)}, bf16[256,256]{0,1:T(8,128)(2,1)S(1)}, u32[]{:S(2)}, u32[]{:S(2)}) collective-permute-start(bf16[256,256]{0,1:T(8,128)(2,1)S(1)} %bitcast.114), channel_id=1, source_target_pairs={{32,0},{40,8},{48,16},{56,24},{64,32},{72,40},{80,48},{88,56},{96,... | collective-permute-start | bytes 393224 | tf_op jit(solution)/shard_map/ppermute | solution.py:17
  309.7 13.2 %collective-permute-start.8 = (bf16[256,256]{0,1:T(8,128)(2,1)S(1)}, bf16[256,256]{0,1:T(8,128)(2,1)S(1)}, u32[]{:S(2)}, u32[]{:S(2)}) collective-permute-start(bf16[256,256]{0,1:T(8,128)(2,1)S(1)} %bitcast.113), channel_id=1, source_target_pairs={{8,0},{16,8},{24,16},{32,24},{40,32},{48,40},{56,48},{64,56},{72,6... | collective-permute-start | bytes 393224 | tf_op jit(solution)/shard_map/ppermute | solution.py:17
  312.6 11.7 %collective-permute-start.10 = (bf16[256,256]{0,1:T(8,128)(2,1)S(1)}, bf16[256,256]{0,1:T(8,128)(2,1)S(1)}, u32[]{:S(2)}, u32[]{:S(2)}) collective-permute-start(bf16[256,256]{0,1:T(8,128)(2,1)S(1)} %bitcast.112), channel_id=1, source_target_pairs={{24,0},{32,8},{40,16},{48,24},{56,32},{64,40},{72,48},{80,56},{88,... | collective-permute-start | bytes 393224 | tf_op jit(solution)/shard_map/ppermute | solution.py:17
  313.9 14.3 %collective-permute-start.9 = (bf16[256,256]{0,1:T(8,128)(2,1)S(1)}, bf16[256,256]{0,1:T(8,128)(2,1)S(1)}, u32[]{:S(2)}, u32[]{:S(2)}) collective-permute-start(bf16[256,256]{0,1:T(8,128)(2,1)S(1)} %bitcast.111), channel_id=1, source_target_pairs={{16,0},{24,8},{32,16},{40,24},{48,32},{56,40},{64,48},{72,56},{80,... | collective-permute-start | bytes 393224 | tf_op jit(solution)/shard_map/ppermute | solution.py:17
  317.9 12.0 %collective-permute-start.12 = (bf16[256,256]{0,1:T(8,128)(2,1)S(1)}, bf16[256,256]{0,1:T(8,128)(2,1)S(1)}, u32[]{:S(2)}, u32[]{:S(2)}) collective-permute-start(bf16[256,256]{0,1:T(8,128)(2,1)S(1)} %bitcast.109), channel_id=1, source_target_pairs={{8,0},{16,8},{24,16},{32,24},{40,32},{48,40},{56,48},{64,56},{72,6... | collective-permute-start | bytes 393224 | tf_op jit(solution)/shard_map/ppermute | solution.py:17
  322.9 7.8 %collective-permute-start.14 = (bf16[256,256]{0,1:T(8,128)(2,1)S(1)}, bf16[256,256]{0,1:T(8,128)(2,1)S(1)}, u32[]{:S(2)}, u32[]{:S(2)}) collective-permute-start(bf16[256,256]{0,1:T(8,128)(2,1)S(1)} %bitcast.108), channel_id=1, source_target_pairs={{24,0},{32,8},{40,16},{48,24},{56,32},{64,40},{72,48},{80,56},{88,... | collective-permute-start | bytes 393224 | tf_op jit(solution)/shard_map/ppermute | solution.py:17
  324.2 8.9 %collective-permute-start.13 = (bf16[256,256]{0,1:T(8,128)(2,1)S(1)}, bf16[256,256]{0,1:T(8,128)(2,1)S(1)}, u32[]{:S(2)}, u32[]{:S(2)}) collective-permute-start(bf16[256,256]{0,1:T(8,128)(2,1)S(1)} %bitcast.107), channel_id=1, source_target_pairs={{16,0},{24,8},{32,16},{40,24},{48,32},{56,40},{64,48},{72,56},{80,... | collective-permute-start | bytes 393224 | tf_op jit(solution)/shard_map/ppermute | solution.py:17
  334.8 287.9 %all-reduce.12.cloned.1.call-start = ((), (), s32[]{:S(2)}) async-start(), calls=%async_computation.2 | async-start | bytes 25296896 | tf_op jit(solution)/shard_map/psum | solution.py:203
  349.7 130.1 %copy-start.6 = (f32[256,2048]{1,0:T(8,128)S(1)}, f32[256,2048]{1,0:T(8,128)}, u32[]{:S(2)}) copy-start(f32[256,2048]{1,0:T(8,128)} %copy-done.4) | copy-start | bytes 6291460
  (42 other events, 161.7 us)
Sparse Core Ops, SparseCore 0:
  67.4 110.0 all-reduce.7
  191.1 103.9 all-reduce.9
  334.9 107.8 all-reduce.13
  446.8 175.7 all-reduce.11
where the time goes:
time: 650 us; the launch traced here: 647 us
  waiting for transfers between devices  456 us (70%)
  starting transfers between devices  47.9 us (7%)
  matrix products  42 us (6%)
  other arithmetic  36.7 us (6%)
  blocking collectives  33.5 us (5%)
  local copies, waits for them, and re-layouts  16.7 us (3%)
  between operations  14.5 us (2%)
    psum x1, waiting for transfers between devices, on_device(): lax.psum(grad_w_query.astype(jnp.bfloat16), 'seq').astype(jnp.float32)  138 us
    psum x1, waiting for transfers between devices, on_device(): hidden = inputs + lax.psum(matmul(heads_out, w_out), 'tp')  110 us
    psum x1, waiting for transfers between devices, on_device(): lax.psum(times_trans(grad_gate_pre, w_gate) + times_trans(grad_up_pre, w_...  101 us
    psum x1, waiting for transfers between devices, on_device(): lax.psum(matmul(activated, w_down).astype(jnp.bfloat16), 'tp')  92.9 us
    ppermute x16, starting transfers between devices, shifted(): lax.ppermute(value, axis, [(source, source + steps) for source in range(f...  47.4 us
    psum x1, blocking collectives, on_device(): lax.psum(grad_gain_attn.astype(jnp.bfloat16), 'seq').astype(jnp.float32)  33.5 us
    ppermute x16, waiting for transfers between devices, shifted(): lax.ppermute(value, axis, [(source, source + steps) for source in range(f...  13.8 us
    dot_general x7, matrix products, outer_sum(): lax.dot_general(left_matrix, right_matrix, (((0,), (0,)), ((), ())), pref...  13.6 us
  transfers between devices with their start and end apart: 20, of which 11 were waited for; matrix products, arithmetic and copies ran while one was open for 5% of the time, Pallas kernels for 0%

commit v1 on v0

v1 whole, which is shorter than its diff:
```python
import jax
import jax.numpy as jnp
from jax import lax
from jax.sharding import PartitionSpec as P

HD = 128
W = 1024
SEQ = 16
TP = 8

epsilon = 1e-06
masked_value = -1e30
low = jnp.bfloat16
wide = jnp.float32


def seq_pairs(step):
    pairs = []
    for x_hi in range(2):
        for y in range(4):
            for core in range(2):
                to_x, to_y, to_core = step(x_hi, y, core)
                pairs.append((x_hi * 8 + y * 2 + core, to_x * 8 + to_y * 2 + to_core))
    return pairs


CORE = seq_pairs(lambda x, y, c: (x, y, 1 - c))
Y_ONE = seq_pairs(lambda x, y, c: (x, y ^ 1, c))
Y_THREE = seq_pairs(lambda x, y, c: (x, y ^ 3, c))
X_HI = seq_pairs(lambda x, y, c: (1 - x, y, c))


def tp_pairs(flip):
    return [(k, k ^ flip) for k in range(TP)]


def shift_pairs(steps):
    return [(k, k + steps) for k in range(SEQ) if 0 <= k + steps < SEQ]


def by_seq(value, pairs):
    return lax.ppermute(value, "seq", pairs)


def by_tp(value, flip):
    return lax.ppermute(value, "tp", tp_pairs(flip))


FLIPS = (5, 7, 3, 4, 6, 2, 1)


def tp_reduce_scatter(partial, tp_index):
    blocks = partial.reshape(TP, partial.shape[0] // TP, partial.shape[1])
    arrived = [
        by_tp(lax.dynamic_index_in_dim(blocks, tp_index ^ flip, 0, False), flip) for flip in FLIPS
    ]
    total = lax.dynamic_index_in_dim(blocks, tp_index, 0, False).astype(wide)
    for piece in arrived:
        total = total + piece.astype(wide)
    return total


def tp_all_gather(rows, tp_index):
    out = jnp.zeros((TP,) + rows.shape, rows.dtype)
    out = lax.dynamic_update_index_in_dim(out, rows, tp_index, 0)
    for flip in FLIPS:
        out = lax.dynamic_update_index_in_dim(out, by_tp(rows, flip), tp_index ^ flip, 0)
    return out.reshape(TP * rows.shape[0], rows.shape[1])


def cut(value, axis, bit):
    size = value.shape[axis] // 2
    first = lax.slice_in_dim(value, 0, size, axis=axis)
    second = lax.slice_in_dim(value, size, 2 * size, axis=axis)
    return jnp.where(bit == 0, first, second)


def join(own, other, axis, bit):
    first = jnp.where(bit == 0, own, other)
    second = jnp.where(bit == 0, other, own)
    return jnp.concatenate([first, second], axis=axis)


def seq_all_reduce(part, axis, bits):
    core, y_gray, y_high, x_hi = bits
    arrived = by_seq(part(1 - core).astype(low), CORE)
    half = part(core) + arrived.astype(wide)
    size = half.shape[axis] // 2
    one = lax.slice_in_dim(half, 0, size, axis=axis)
    two = lax.slice_in_dim(half, size, 2 * size, axis=axis)
    arrived = (
        by_seq(cut(one, axis, 1 - y_gray).astype(low), Y_ONE),
        by_seq(cut(two, axis, 1 - y_high).astype(low), Y_THREE),
    )
    one = cut(one, axis, y_gray) + arrived[0].astype(wide)
    two = cut(two, axis, y_high) + arrived[1].astype(wide)
    arrived = (
        by_seq(cut(one, axis, 1 - y_high).astype(low), Y_THREE),
        by_seq(cut(two, axis, 1 - y_gray).astype(low), Y_ONE),
    )
    one = cut(one, axis, y_high) + arrived[0].astype(wide)
    two = cut(two, axis, y_gray) + arrived[1].astype(wide)
    arrived = by_seq(jnp.where(x_hi == 0, two, one).astype(low), X_HI)
    own = (jnp.where(x_hi == 0, one, two) + arrived.astype(wide)).astype(low)
    arrived = by_seq(own, X_HI)
    one = jnp.where(x_hi == 0, own, arrived)
    two = jnp.where(x_hi == 0, arrived, own)
    arrived = (by_seq(one, Y_THREE), by_seq(two, Y_ONE))
    one = join(one, arrived[0], axis, y_high)
    two = join(two, arrived[1], axis, y_gray)
    arrived = (by_seq(one, Y_ONE), by_seq(two, Y_THREE))
    one = join(one, arrived[0], axis, y_gray)
    two = join(two, arrived[1], axis, y_high)
    half = jnp.concatenate([one, two], axis=axis)
    return join(half, by_seq(half, CORE), axis, core).astype(wide)


def sum_everywhere(value):
    for pairs in (CORE, Y_ONE, Y_THREE, X_HI):
        value = value + by_seq(value, pairs)
    for flip in (2, 6, 1):
        value = value + by_tp(value, flip)
    return value


def rms_factor(field_rows):
    return lax.rsqrt(jnp.mean(field_rows * field_rows, axis=-1, keepdims=True) + epsilon)


def norm_back(grad_normed, unit_rows, factor, gain_vec):
    scaled = grad_normed * gain_vec
    return factor * (scaled - unit_rows * jnp.mean(scaled * unit_rows, axis=-1, keepdims=True))


def matmul(left_matrix, right_matrix):
    return jnp.dot(left_matrix, right_matrix, preferred_element_type=wide)


def outer_sum(left_matrix, right_matrix):
    return lax.dot_general(
        left_matrix, right_matrix, (((0,), (0,)), ((), ())), preferred_element_type=wide
    )


def times_trans(left_matrix, right_matrix):
    return lax.dot_general(
        left_matrix, right_matrix, (((1,), (1,)), ((), ())), preferred_element_type=wide
    )


def neighbours(own, core, way):
    two = by_seq(own, shift_pairs(2 * way))
    four = by_seq(own, shift_pairs(4 * way))
    sends_own = core == (0 if way == 1 else 1)
    across = by_seq(jnp.concatenate([two, jnp.where(sends_own, own, four)], axis=0), CORE)
    return jnp.concatenate([own, two, across[: own.shape[0]], four, across[own.shape[0] :]], axis=0)


def distances(core, way):
    near_first = core == (0 if way == 1 else 1)
    return jnp.stack(
        [
            jnp.int32(0),
            jnp.int32(2),
            jnp.where(near_first, 1, 3).astype(jnp.int32),
            jnp.int32(4),
            jnp.where(near_first, 3, 1).astype(jnp.int32),
        ]
    )


def seen(query_pos, key_pos):
    return (
        (key_pos[None, :] >= 0)
        & (query_pos[:, None] < SEQ * 256)
        & (key_pos[None, :] <= query_pos[:, None])
        & (key_pos[None, :] > query_pos[:, None] - W)
    )


def split_three(value):
    first = value.astype(low)
    rest = value - first.astype(wide)
    second = rest.astype(low)
    third = (rest - second.astype(wide)).astype(low)
    return first, second, third


def on_device(
    tokens, gain_attn, w_query, w_key, w_value, w_out, gain_ffn, w_gate, w_up, w_down, cotangent
):
    rows = tokens.shape[0]
    width = tokens.shape[1]
    heads = w_query.shape[1] // HD
    features = heads * HD
    score_scale = HD ** (-0.5)
    seq_index = lax.axis_index("seq")
    tp_index = lax.axis_index("tp")
    core = seq_index & 1
    y_low = (seq_index >> 1) & 1
    y_high = (seq_index >> 2) & 1
    x_hi = seq_index >> 3
    bits = (core, y_low ^ y_high, y_high, x_hi)
    share = rows // TP

    def own_share(value):
        return lax.dynamic_slice_in_dim(value, tp_index * share, share, 0)

    inputs = tokens.astype(wide)
    factor_attn = rms_factor(inputs)
    unit_attn = inputs * factor_attn
    normed_attn = (unit_attn * gain_attn).astype(low)
    key_rows = matmul(normed_attn, w_key).astype(low)
    value_rows = matmul(normed_attn, w_value).astype(low)
    key_value = neighbours(jnp.concatenate([key_rows, value_rows], axis=1), core, 1)
    query_rows = matmul(normed_attn, w_query).astype(low)

    own_pos = seq_index * rows + jnp.arange(rows, dtype=jnp.int32)
    key_pos = (
        (seq_index - distances(core, 1))[:, None] * rows + jnp.arange(rows, dtype=jnp.int32)[None]
    ).reshape(-1)
    later_pos = (
        (seq_index + distances(core, -1))[:, None] * rows + jnp.arange(rows, dtype=jnp.int32)[None]
    ).reshape(-1)
    allowed = seen(own_pos, key_pos)
    allowed_later = seen(later_pos, own_pos)

    queries = query_rows.reshape(rows, heads, HD)
    key_all = key_value[:, :features].reshape(-1, heads, HD)
    value_all = key_value[:, features:].reshape(-1, heads, HD)

    def scores_of(query_part, key_part, mask):
        scores = (
            jnp.einsum("ihd,chd->hic", query_part, key_part, preferred_element_type=wide)
            * score_scale
        )
        return jnp.where(mask[None], scores, masked_value)

    scores = scores_of(queries, key_all, allowed)
    row_peak = jnp.max(scores, axis=-1, keepdims=True)
    log_total = row_peak + jnp.log(jnp.sum(jnp.exp(scores - row_peak), axis=-1, keepdims=True))
    weights_low = jnp.exp(scores - log_total).astype(low)
    mixed = jnp.einsum("hic,chd->ihd", weights_low, value_all, preferred_element_type=wide)
    heads_out = mixed.reshape(rows, -1).astype(low)

    attn_sum = tp_reduce_scatter(matmul(heads_out, w_out).astype(low), tp_index)
    hidden = own_share(inputs) + attn_sum
    factor_ffn = rms_factor(hidden)
    unit_ffn = hidden * factor_ffn
    normed_ffn = tp_all_gather((unit_ffn * gain_ffn).astype(low), tp_index)

    log_parts = split_three(log_total[:, :, 0])
    log_cols = jnp.concatenate([part.T for part in log_parts], axis=1)
    log_cols = jnp.pad(log_cols, ((0, 0), (0, HD - log_cols.shape[1])))
    query_side = neighbours(
        jnp.concatenate([query_rows, heads_out, log_cols], axis=1), core, -1
    )

    gate_pre = matmul(normed_ffn, w_gate)
    up_pre = matmul(normed_ffn, w_up)
    gate_sigmoid = jax.nn.sigmoid(gate_pre)
    gate_silu = gate_pre * gate_sigmoid
    activated = (gate_silu * up_pre).astype(low)
    grad_act = times_trans(cotangent, w_down)
    grad_gate = (
        grad_act * up_pre * gate_sigmoid * (1.0 + gate_pre * (1.0 - gate_sigmoid))
    ).astype(low)
    grad_up = (grad_act * gate_silu).astype(low)
    grad_normed_ffn = tp_reduce_scatter(
        (times_trans(grad_gate, w_gate) + times_trans(grad_up, w_up)).astype(low), tp_index
    )

    def down_part(bit):
        return outer_sum(activated, cut(cotangent, 1, bit))

    def gate_up_part(bit):
        side = cut(normed_ffn, 1, bit)
        return jnp.concatenate([outer_sum(grad_gate, side), outer_sum(grad_up, side)], axis=0)

    grad_w_down = seq_all_reduce(down_part, 1, bits)
    grad_gate_up = seq_all_reduce(gate_up_part, 1, bits)

    ffn_sum = tp_reduce_scatter(matmul(activated, w_down).astype(low), tp_index)
    block_out = tp_all_gather((hidden + ffn_sum).astype(low), tp_index)

    gain_ffn_part = jnp.sum(grad_normed_ffn * unit_ffn, axis=0)
    grad_hidden = own_share(cotangent).astype(wide) + norm_back(
        grad_normed_ffn, unit_ffn, factor_ffn, gain_ffn
    )
    grad_hidden_low = tp_all_gather(grad_hidden.astype(low), tp_index)
    grad_heads_rows = times_trans(grad_hidden_low, w_out).astype(low)
    grad_heads_all = neighbours(grad_heads_rows, core, -1).reshape(-1, heads, HD)
    grad_heads = grad_heads_rows.reshape(rows, heads, HD)

    inner = jnp.sum(
        grad_heads.astype(wide) * heads_out.reshape(rows, heads, HD).astype(wide), axis=-1
    )
    weights = jnp.exp(scores_of(queries, key_all, allowed) - log_total)
    grad_probs = jnp.einsum("ihd,chd->hic", grad_heads, value_all, preferred_element_type=wide)
    grad_scores = (weights * (grad_probs - inner.T[:, :, None])).astype(low)
    grad_query = (
        jnp.einsum("hic,chd->ihd", grad_scores, key_all, preferred_element_type=wide) * score_scale
    )
    grad_query = grad_query.reshape(rows, -1).astype(low)

    query_all = query_side[:, :features].reshape(-1, heads, HD)
    mixed_all = query_side[:, features : 2 * features].reshape(-1, heads, HD)
    logs = query_side[:, 2 * features : 2 * features + 3 * heads].astype(wide)
    log_all = logs[:, :heads] + logs[:, heads : 2 * heads] + logs[:, 2 * heads :]
    inner_all = jnp.sum(grad_heads_all.astype(wide) * mixed_all.astype(wide), axis=-1)
    own_keys = key_rows.reshape(rows, heads, HD)
    own_values = value_rows.reshape(rows, heads, HD)
    weights_later = jnp.exp(
        scores_of(query_all, own_keys, allowed_later) - log_all.T[:, :, None]
    )
    grad_value = jnp.einsum(
        "hic,ihd->chd", weights_later.astype(low), grad_heads_all, preferred_element_type=wide
    )
    grad_probs_later = jnp.einsum(
        "ihd,chd->hic", grad_heads_all, own_values, preferred_element_type=wide
    )
    grad_scores_later = (weights_later * (grad_probs_later - inner_all.T[:, :, None])).astype(low)
    grad_key = (
        jnp.einsum("hic,ihd->chd", grad_scores_later, query_all, preferred_element_type=wide)
        * score_scale
    )
    grad_key = grad_key.reshape(rows, -1).astype(low)
    grad_value = grad_value.reshape(rows, -1).astype(low)

    grad_qkv = jnp.concatenate([grad_query, grad_key, grad_value], axis=1)

    def attn_part(bit):
        return jnp.concatenate(
            [
                outer_sum(cut(normed_attn, 1, bit), grad_qkv),
                outer_sum(cut(grad_hidden_low, 1, bit), heads_out),
            ],
            axis=1,
        )

    local_back = (
        times_trans(grad_query, w_query)
        + times_trans(grad_key, w_key)
        + times_trans(grad_value, w_value)
    )
    grad_normed_attn = tp_reduce_scatter(local_back.astype(low), tp_index)
    gain_attn_part = jnp.sum(local_back * unit_attn, axis=0)
    grad_attn = seq_all_reduce(attn_part, 0, bits)

    gains = sum_everywhere(jnp.stack([gain_attn_part, gain_ffn_part]))
    gains = lax.dynamic_slice_in_dim(gains, tp_index * (width // TP), width // TP, 1)

    grad_tokens = grad_hidden + norm_back(
        grad_normed_attn, own_share(unit_attn), own_share(factor_attn), gain_attn
    )
    grad_tokens = tp_all_gather(grad_tokens.astype(low), tp_index).astype(wide)
    hidden_units = w_gate.shape[1]
    return (
        block_out,
        grad_tokens,
        gains[0],
        grad_attn[:, :features],
        grad_attn[:, features : 2 * features],
        grad_attn[:, 2 * features : 3 * features],
        grad_attn[:, 3 * features :].T,
        gains[1],
        grad_gate_up[:hidden_units].T,
        grad_gate_up[hidden_units:].T,
        grad_w_down,
    )


def solution(mesh):
    return jax.shard_map(
        on_device,
        mesh=mesh,
        in_specs=(
            P("seq", None),
            P(),
            P(None, "tp"),
            P(None, "tp"),
            P(None, "tp"),
            P("tp", None),
            P(),
            P(None, "tp"),
            P(None, "tp"),
            P("tp", None),
            P("seq", None),
        ),
        out_specs=(
            P("seq", None),
            P("seq", None),
            P("tp"),
            P(None, "tp"),
            P(None, "tp"),
            P(None, "tp"),
            P("tp", None),
            P("tp"),
            P(None, "tp"),
            P(None, "tp"),
            P("tp", None),
        ),
        check_vma=False,
    )
```

time: 650 us -> 474 us (0.73)
  waiting for transfers between devices: 456 us -> 133 us
  starting transfers between devices: 47.9 us -> 203 us
  blocking collectives: 33.5 us -> 0 us
  local copies, waits for them, and re-layouts: 16.7 us -> 42.4 us
  between operations: 14.5 us -> 2.7 us
  other arithmetic: 36.7 us -> 48.1 us
    psum x4 -> x0, waiting for transfers between devices: 442 us -> none  [the longest x1 138 us: on_device(): lax.psum(grad_w_query.astype(jnp.bfloat16), 'seq').astype(jnp.float32)]
    ppermute x16 -> x108, starting transfers between devices: 47.4 us -> 203 us  [the longest x49 130 us: by_seq(): return lax.ppermute(value, 'seq', pairs)]
    ppermute x16 -> x108, waiting for transfers between devices: 13.8 us -> 133 us  [the longest x49 80.3 us: by_seq(): return lax.ppermute(value, 'seq', pairs)]
    psum x1 -> x0, blocking collectives: 33.5 us -> none  [on_device(): lax.psum(grad_gain_attn.astype(jnp.bfloat16), 'seq').astype(jnp.float32)]
    transpose x0 -> x2, local copies, waits for them, and re-layouts: none -> 13.4 us  [the longest x1 10.6 us: on_device(): grad_gate_up[hidden_units:]]
    concatenate x0 -> x17, other arithmetic: none -> 9.13 us  [the longest x3 2.87 us: neighbours(): jnp.concatenate([two, jnp.where(sends_own, own, four)], axis=0)]
    select_n x0 -> x21, other arithmetic: none -> 8.52 us  [the longest x15 6.25 us: join(): first = jnp.where(bit == 0, own, other)]
    dynamic_update_slice x0 -> x28, local copies, waits for them, and re-layouts: none -> 6.82 us  [tp_all_gather(): lax.dynamic_update_index_in_dim(out, by_tp(rows, flip), tp_index ^ flip, 0)]
  transfers between devices with their start and end apart: 20 -> 108, of which waited for: 11 -> 49; matrix products, arithmetic and copies ran while one was open for 5% -> 19% of each run, Pallas kernels for 0% -> 0%
where the time goes in v1:
time: 474 us; the launch traced here: 465 us
  starting transfers between devices  203 us (43%)
  waiting for transfers between devices  133 us (28%)
  other arithmetic  48.1 us (10%)
  local copies, waits for them, and re-layouts  42.4 us (9%)
  matrix products  36.3 us (8%)
    ppermute x49, starting transfers between devices, by_seq(): return lax.ppermute(value, 'seq', pairs)  130 us
    ppermute x49, waiting for transfers between devices, by_seq(): return lax.ppermute(value, 'seq', pairs)  80.3 us
    ppermute x59, starting transfers between devices, by_tp(): return lax.ppermute(value, 'tp', tp_pairs(flip))  73.2 us
    ppermute x59, waiting for transfers between devices, by_tp(): return lax.ppermute(value, 'tp', tp_pairs(flip))  52.3 us
    unnamed x114, local copies, waits for them, and re-layouts  17.5 us
    dot_general x7, matrix products, times_trans(): lax.dot_general(left_matrix, right_matrix, (((1,), (1,)), ((), ())), pref...  11.4 us
    transpose x1, local copies, waits for them, and re-layouts, on_device(): grad_gate_up[hidden_units:]  10.6 us
    convert_element_type x3, other arithmetic, seq_all_reduce(): return join(half, by_seq(half, CORE), axis, core).astype(wide)  9.92 us
  transfers between devices with their start and end apart: 108, of which 49 were waited for; matrix products, arithmetic and copies ran while one was open for 19% of the time, Pallas kernels for 0%

profile of v1, /device:TPU:1, one launch (start us, length us, event | category | flops | bytes accessed | tf_op | source)
XLA Modules:
  0.0 465.3 jit_solution(10611563208425359275)
XLA Ops:
  6.3 6.4 %collective-permute-start.1 = (bf16[256,512]{0,1:T(8,128)(2,1)}, bf16[256,512]{0,1:T(8,128)(2,1)}, u32[]{:S(2)}, u32[]{:S(2)}) collective-permute-start(bf16[256,512]{0,1:T(8,128)(2,1)} %pad_maximum_fusion.15), channel_id=1, source_target_pairs={{0,32},{8,40},{16,48},{24,56},{32,64},{40,72},{48,80},{56,88},{64,... | collective-permute-start | bytes 786440 | tf_op jit(solution)/shard_map/ppermute | solution.py:42
  114.1 8.6 %collective-permute-start.47 = (bf16[512,640]{0,1:T(8,128)(2,1)}, bf16[512,640]{0,1:T(8,128)(2,1)}, u32[]{:S(2)}, u32[]{:S(2)}) collective-permute-start(bf16[512,640]{0,1:T(8,128)(2,1)} %pad_maximum_fusion.7), channel_id=1, source_target_pairs={{0,8},{8,0},{16,24},{24,16},{32,40},{40,32},{48,56},{56,48},{64,72... | collective-permute-start | bytes 1966088 | tf_op jit(solution)/shard_map/ppermute | solution.py:42
  144.6 4.1 collective-permute-done.39
  154.5 4.8 %collective-permute-done.41 = bf16[32,2048]{1,0:T(8,128)(2,1)S(1)} collective-permute-done((bf16[32,2048]{1,0:T(8,128)(2,1)S(1)}, bf16[32,2048]{1,0:T(8,128)(2,1)S(1)}, u32[]{:S(2)}, u32[]{:S(2)}) %collective-permute-start.41) | collective-permute-done | bytes 131104 | tf_op jit(solution)/shard_map/ppermute | solution.py:46
  160.9 4.4 collective-permute-done.42
  165.3 4.1 collective-permute-done.43
  187.5 8.8 %collective-permute-start.50 = (bf16[512,256]{0,1:T(8,128)(2,1)S(1)}, bf16[512,256]{0,1:T(8,128)(2,1)S(1)}, u32[]{:S(2)}, u32[]{:S(2)}) collective-permute-start(bf16[512,256]{0,1:T(8,128)(2,1)S(1)} %pad_maximum_fusion.16), channel_id=1, source_target_pairs={{0,8},{8,0},{16,24},{24,16},{32,40},{40,32},{48,56},{56,48},{64,72... | collective-permute-start | bytes 786440 | tf_op jit(solution)/shard_map/ppermute | solution.py:42
  217.4 16.5 %collective-permute-start.67 = (f32[2,2048]{1,0:T(2,128)S(1)}, f32[2,2048]{1,0:T(2,128)S(1)}, u32[]{:S(2)}, u32[]{:S(2)}) collective-permute-start(f32[2,2048]{1,0:T(2,128)S(1)} %fusion.167), channel_id=1, source_target_pairs={{0,48},{8,56},{16,32},{24,40},{32,16},{40,24},{48,0},{56,8},{64,11... | collective-permute-start | bytes 49160 | tf_op jit(solution)/shard_map/ppermute | solution.py:42
  254.9 7.8 %collective-permute-start.84 = (bf16[1376,1024]{1,0:T(8,128)(2,1)S(1)}, bf16[1376,1024]{1,0:T(8,128)(2,1)S(1)}, u32[]{:S(2)}, u32[]{:S(2)}) collective-permute-start(bf16[1376,1024]{1,0:T(8,128)(2,1)S(1)} %copy-done.20), channel_id=1, source_target_pairs={{0,8},{8,0},{16,24},{24,16},{32,40},{40,32},{48,56},{56,48},{64,72... | collective-permute-start | bytes 8454152 | tf_op jit(solution)/shard_map/ppermute | solution.py:42
  277.3 4.8 %collective-permute-done.99 = bf16[688,256]{1,0:T(8,128)(2,1)S(1)} collective-permute-done((bf16[688,256]{1,0:T(8,128)(2,1)S(1)}, bf16[688,256]{1,0:T(8,128)(2,1)S(1)}, u32[]{:S(2)}, u32[]{:S(2)}) %collective-permute-start.99) | collective-permute-done | bytes 352288 | tf_op jit(solution)/shard_map/ppermute | solution.py:42
  286.7 4.3 collective-permute-done.98
  297.4 4.0 collective-permute-done.101
  315.3 4.7 %collective-permute-done.106 = bf16[688,256]{1,0:T(8,128)(2,1)S(1)} collective-permute-done((bf16[688,256]{1,0:T(8,128)(2,1)S(1)}, bf16[688,256]{1,0:T(8,128)(2,1)S(1)}, u32[]{:S(2)}, u32[]{:S(2)}) %collective-permute-start.106) | collective-permute-done | bytes 352288 | tf_op jit(solution)/shard_map/ppermute | solution.py:42
  326.4 7.9 %collective-permute-done.75 = bf16[256,1024]{0,1:T(8,128)(2,1)S(1)} collective-permute-done((bf16[256,1024]{0,1:T(8,128)(2,1)S(1)}, bf16[256,1024]{0,1:T(8,128)(2,1)S(1)}, u32[]{:S(2)}, u32[]{:S(2)}) %collective-permute-start.75) | collective-permute-done | bytes 524320 | tf_op jit(solution)/shard_map/ppermute | solution.py:42
  337.3 6.4 %collective-permute-done.87 = bf16[1376,256]{1,0:T(8,128)(2,1)S(1)} collective-permute-done((bf16[1376,256]{1,0:T(8,128)(2,1)S(1)}, bf16[1376,256]{1,0:T(8,128)(2,1)S(1)}, u32[]{:S(2)}, u32[]{:S(2)}) %collective-permute-start.87) | collective-permute-done | bytes 704544 | tf_op jit(solution)/shard_map/ppermute | solution.py:42
  352.0 3.8 collective-permute-done.77
  363.1 16.4 %collective-permute-start.107 = (bf16[688,1024]{1,0:T(8,128)(2,1)S(1)}, bf16[688,1024]{1,0:T(8,128)(2,1)S(1)}, u32[]{:S(2)}, u32[]{:S(2)}) collective-permute-start(bf16[688,1024]{1,0:T(8,128)(2,1)S(1)} %pad_maximum_fusion.4), channel_id=1, source_target_pairs={{0,8},{8,0},{16,24},{24,16},{32,40},{40,32},{48,56},{56,48},{64,72... | collective-permute-start | bytes 4227080 | tf_op jit(solution)/shard_map/ppermute | solution.py:42
  391.3 5.2 %collective-permute-done.82 = bf16[256,1024]{0,1:T(8,128)(2,1)S(1)} collective-permute-done((bf16[256,1024]{0,1:T(8,128)(2,1)S(1)}, bf16[256,1024]{0,1:T(8,128)(2,1)S(1)}, u32[]{:S(2)}, u32[]{:S(2)}) %collective-permute-start.82) | collective-permute-done | bytes 524320 | tf_op jit(solution)/shard_map/ppermute | solution.py:42
  397.0 4.5 collective-permute-done.93
  407.0 7.4 %collective-permute-start.83 = (bf16[1024,1024]{0,1:T(8,128)(2,1)S(1)}, bf16[1024,1024]{0,1:T(8,128)(2,1)S(1)}, u32[]{:S(2)}, u32[]{:S(2)}) collective-permute-start(bf16[1024,1024]{0,1:T(8,128)(2,1)S(1)} %pad_maximum_fusion.3), channel_id=1, source_target_pairs={{0,8},{8,0},{16,24},{24,16},{32,40},{40,32},{48,56},{56,48},{64,72... | collective-permute-start | bytes 6291464 | tf_op jit(solution)/shard_map/ppermute | solution.py:42
  414.4 6.3 %collective-permute-done.94 = bf16[1376,256]{1,0:T(8,128)(2,1)S(1)} collective-permute-done((bf16[1376,256]{1,0:T(8,128)(2,1)S(1)}, bf16[1376,256]{1,0:T(8,128)(2,1)S(1)}, u32[]{:S(2)}, u32[]{:S(2)}) %collective-permute-start.94) | collective-permute-done | bytes 704544 | tf_op jit(solution)/shard_map/ppermute | solution.py:42
  423.3 4.3 collective-permute-start.95
  448.6 5.7 %maximum_convert_fusion = f32[1376,2048]{1,0:T(8,128)} fusion(bf16[1376,1024]{1,0:T(8,128)(2,1)S(1)} %get-tuple-element.46, bf16[1376,1024]{1,0:T(8,128)(2,1)S(1)} %get-tuple-element.45), kind=kLoop, calls=%fused_computation.3 | loop fusion | flops 11272192 | bytes 16908288 | tf_op jit(solution)/shard_map/convert_element_type | solution.py:115
  454.2 10.6 %slice_bitcast_fusion = (f32[2048,688]{0,1:T(8,128)}, f32[2048,688]{0,1:T(8,128)}) fusion(f32[1376,2048]{1,0:T(8,128)} %maximum_convert_fusion), kind=kLoop, calls=%fused_computation | loop fusion | bytes 22544384 | tf_op jit(solution)/shard_map/transpose | solution.py:368
  (486 shorter events, 301.0 us)
Async XLA Ops:
  60.0 34.7 %collective-permute-start.46 = (bf16[256,640]{0,1:T(8,128)(2,1)S(1)}, bf16[256,640]{0,1:T(8,128)(2,1)S(1)}, u32[]{:S(2)}, u32[]{:S(2)}) collective-permute-start(bf16[256,640]{0,1:T(8,128)(2,1)S(1)} %pad_maximum_fusion.14), channel_id=1, source_target_pairs={{32,0},{40,8},{48,16},{56,24},{64,32},{72,40},{80,48},{88,56},{96,... | collective-permute-start | bytes 983048 | tf_op jit(solution)/shard_map/ppermute | solution.py:42
  61.3 35.2 %collective-permute-start.45 = (bf16[256,640]{0,1:T(8,128)(2,1)S(1)}, bf16[256,640]{0,1:T(8,128)(2,1)S(1)}, u32[]{:S(2)}, u32[]{:S(2)}) collective-permute-start(bf16[256,640]{0,1:T(8,128)(2,1)S(1)} %pad_maximum_fusion.14), channel_id=1, source_target_pairs={{16,0},{24,8},{32,16},{40,24},{48,32},{56,40},{64,48},{72,56},{80,... | collective-permute-start | bytes 983048 | tf_op jit(solution)/shard_map/ppermute | solution.py:42
  106.4 16.2 %collective-permute-start.34 = (bf16[32,2048]{1,0:T(8,128)(2,1)S(1)}, bf16[32,2048]{1,0:T(8,128)(2,1)S(1)}, u32[]{:S(2)}, u32[]{:S(2)}) collective-permute-start(bf16[32,2048]{1,0:T(8,128)(2,1)S(1)} %get-tuple-element.92), channel_id=1, source_target_pairs={{0,4},{1,5},{2,6},{3,7},{4,0},{5,1},{6,2},{7,3},{8,12},{9,13},{10,... | collective-permute-start | bytes 393224 | tf_op jit(solution)/shard_map/ppermute | solution.py:46
  107.7 18.2 %collective-permute-start.33 = (bf16[32,2048]{1,0:T(8,128)(2,1)S(1)}, bf16[32,2048]{1,0:T(8,128)(2,1)S(1)}, u32[]{:S(2)}, u32[]{:S(2)}) collective-permute-start(bf16[32,2048]{1,0:T(8,128)(2,1)S(1)} %get-tuple-element.93), channel_id=1, source_target_pairs={{0,3},{1,2},{2,1},{3,0},{4,7},{5,6},{6,5},{7,4},{8,11},{9,10},{10,... | collective-permute-start | bytes 393224 | tf_op jit(solution)/shard_map/ppermute | solution.py:46
  108.3 19.6 %collective-permute-start.32 = (bf16[32,2048]{1,0:T(8,128)(2,1)S(1)}, bf16[32,2048]{1,0:T(8,128)(2,1)S(1)}, u32[]{:S(2)}, u32[]{:S(2)}) collective-permute-start(bf16[32,2048]{1,0:T(8,128)(2,1)S(1)} %get-tuple-element.94), channel_id=1, source_target_pairs={{0,7},{1,6},{2,5},{3,4},{4,3},{5,2},{6,1},{7,0},{8,15},{9,14},{10,... | collective-permute-start | bytes 393224 | tf_op jit(solution)/shard_map/ppermute | solution.py:46
  110.6 17.4 %collective-permute-start.31 = (bf16[32,2048]{1,0:T(8,128)(2,1)S(1)}, bf16[32,2048]{1,0:T(8,128)(2,1)S(1)}, u32[]{:S(2)}, u32[]{:S(2)}) collective-permute-start(bf16[32,2048]{1,0:T(8,128)(2,1)S(1)} %get-tuple-element.88), channel_id=1, source_target_pairs={{0,5},{1,4},{2,7},{3,6},{4,1},{5,0},{6,3},{7,2},{8,13},{9,12},{10,... | collective-permute-start | bytes 393224 | tf_op jit(solution)/shard_map/ppermute | solution.py:46
  114.1 87.2 %collective-permute-start.47 = (bf16[512,640]{0,1:T(8,128)(2,1)}, bf16[512,640]{0,1:T(8,128)(2,1)}, u32[]{:S(2)}, u32[]{:S(2)}) collective-permute-start(bf16[512,640]{0,1:T(8,128)(2,1)} %pad_maximum_fusion.7), channel_id=1, source_target_pairs={{0,8},{8,0},{16,24},{24,16},{32,40},{40,32},{48,56},{56,48},{64,72... | collective-permute-start | bytes 1966088 | tf_op jit(solution)/shard_map/ppermute | solution.py:42
  127.9 48.3 %collective-permute-start.27 = (bf16[32,2048]{1,0:T(8,128)(2,1)}, bf16[32,2048]{1,0:T(8,128)(2,1)S(1)}, u32[]{:S(2)}, u32[]{:S(2)}) collective-permute-start(bf16[32,2048]{1,0:T(8,128)(2,1)} %get-tuple-element.34), channel_id=1, source_target_pairs={{0,4},{1,5},{2,6},{3,7},{4,0},{5,1},{6,2},{7,3},{8,12},{9,13},{10,... | collective-permute-start | bytes 393224 | tf_op jit(solution)/shard_map/ppermute | solution.py:46
  131.6 46.6 %collective-permute-start.28 = (bf16[32,2048]{1,0:T(8,128)(2,1)}, bf16[32,2048]{1,0:T(8,128)(2,1)S(1)}, u32[]{:S(2)}, u32[]{:S(2)}) collective-permute-start(bf16[32,2048]{1,0:T(8,128)(2,1)} %get-tuple-element.34), channel_id=1, source_target_pairs={{0,6},{1,7},{2,4},{3,5},{4,2},{5,3},{6,0},{7,1},{8,14},{9,15},{10,... | collective-permute-start | bytes 393224 | tf_op jit(solution)/shard_map/ppermute | solution.py:46
  135.4 77.1 %collective-permute-start.29 = (bf16[32,2048]{1,0:T(8,128)(2,1)}, bf16[32,2048]{1,0:T(8,128)(2,1)}, u32[]{:S(2)}, u32[]{:S(2)}) collective-permute-start(bf16[32,2048]{1,0:T(8,128)(2,1)} %get-tuple-element.34), channel_id=1, source_target_pairs={{0,2},{1,3},{2,0},{3,1},{4,6},{5,7},{6,4},{7,5},{8,10},{9,11},{10,... | collective-permute-start | bytes 393224 | tf_op jit(solution)/shard_map/ppermute | solution.py:46
  173.2 42.6 %collective-permute-start.30 = (bf16[32,2048]{1,0:T(8,128)(2,1)}, bf16[32,2048]{1,0:T(8,128)(2,1)}, u32[]{:S(2)}, u32[]{:S(2)}) collective-permute-start(bf16[32,2048]{1,0:T(8,128)(2,1)} %get-tuple-element.34), channel_id=1, source_target_pairs={{0,1},{1,0},{2,3},{3,2},{4,5},{5,4},{6,7},{7,6},{8,9},{9,8},{10,11... | collective-permute-start | bytes 393224 | tf_op jit(solution)/shard_map/ppermute | solution.py:46
  217.4 17.6 %collective-permute-start.67 = (f32[2,2048]{1,0:T(2,128)S(1)}, f32[2,2048]{1,0:T(2,128)S(1)}, u32[]{:S(2)}, u32[]{:S(2)}) collective-permute-start(f32[2,2048]{1,0:T(2,128)S(1)} %fusion.167), channel_id=1, source_target_pairs={{0,48},{8,56},{16,32},{24,40},{32,16},{40,24},{48,0},{56,8},{64,11... | collective-permute-start | bytes 49160 | tf_op jit(solution)/shard_map/ppermute | solution.py:42
  254.9 68.1 %collective-permute-start.84 = (bf16[1376,1024]{1,0:T(8,128)(2,1)S(1)}, bf16[1376,1024]{1,0:T(8,128)(2,1)S(1)}, u32[]{:S(2)}, u32[]{:S(2)}) collective-permute-start(bf16[1376,1024]{1,0:T(8,128)(2,1)S(1)} %copy-done.20), channel_id=1, source_target_pairs={{0,8},{8,0},{16,24},{24,16},{32,40},{40,32},{48,56},{56,48},{64,72... | collective-permute-start | bytes 8454152 | tf_op jit(solution)/shard_map/ppermute | solution.py:42
  263.8 56.3 %collective-permute-start.72 = (bf16[1024,1024]{0,1:T(8,128)(2,1)S(1)}, bf16[1024,1024]{0,1:T(8,128)(2,1)S(1)}, u32[]{:S(2)}, u32[]{:S(2)}) collective-permute-start(bf16[1024,1024]{0,1:T(8,128)(2,1)S(1)} %pad_maximum_fusion.2), channel_id=1, source_target_pairs={{0,8},{8,0},{16,24},{24,16},{32,40},{40,32},{48,56},{56,48},{64,72... | collective-permute-start | bytes 6291464 | tf_op jit(solution)/shard_map/ppermute | solution.py:42
  315.1 36.7 %collective-permute-start.104 = (bf16[688,256]{1,0:T(8,128)(2,1)}, bf16[688,256]{1,0:T(8,128)(2,1)S(1)}, u32[]{:S(2)}, u32[]{:S(2)}) collective-permute-start(bf16[688,256]{1,0:T(8,128)(2,1)} %pad_maximum_fusion.12), channel_id=1, source_target_pairs={{0,16},{8,24},{16,0},{24,8},{32,48},{40,56},{48,32},{56,40},{64,80... | collective-permute-start | bytes 1056776 | tf_op jit(solution)/shard_map/ppermute | solution.py:42
  324.5 19.2 %collective-permute-start.87 = (bf16[1376,256]{1,0:T(8,128)(2,1)S(1)}, bf16[1376,256]{1,0:T(8,128)(2,1)S(1)}, u32[]{:S(2)}, u32[]{:S(2)}) collective-permute-start(bf16[1376,256]{1,0:T(8,128)(2,1)S(1)} %get-tuple-element.49), channel_id=1, source_target_pairs={{0,48},{8,56},{16,32},{24,40},{32,16},{40,24},{48,0},{56,8},{64,11... | collective-permute-start | bytes 2113544 | tf_op jit(solution)/shard_map/ppermute | solution.py:42
  326.3 17.4 %collective-permute-start.85 = (bf16[1376,256]{1,0:T(8,128)(2,1)S(1)}, bf16[1376,256]{1,0:T(8,128)(2,1)S(1)}, u32[]{:S(2)}, u32[]{:S(2)}) collective-permute-start(bf16[1376,256]{1,0:T(8,128)(2,1)S(1)} %get-tuple-element.50), channel_id=1, source_target_pairs={{0,16},{8,24},{16,0},{24,8},{32,48},{40,56},{48,32},{56,40},{64,80... | collective-permute-start | bytes 2113544 | tf_op jit(solution)/shard_map/ppermute | solution.py:42
  356.1 23.3 %collective-permute-start.78 = (bf16[128,1024]{0,1:T(8,128)(2,1)S(1)}, bf16[128,1024]{0,1:T(8,128)(2,1)S(1)}, u32[]{:S(2)}, u32[]{:S(2)}) collective-permute-start(bf16[128,1024]{0,1:T(8,128)(2,1)S(1)} %add_convert_fusion.1), channel_id=1, source_target_pairs={{0,64},{8,72},{16,80},{24,88},{32,96},{40,104},{48,112},{56,120},{... | collective-permute-start | bytes 786440 | tf_op jit(solution)/shard_map/ppermute | solution.py:42
  362.4 18.3 %collective-permute-start.89 = (bf16[1376,128]{1,0:T(8,128)(2,1)S(1)}, bf16[1376,128]{1,0:T(8,128)(2,1)S(1)}, u32[]{:S(2)}, u32[]{:S(2)}) collective-permute-start(bf16[1376,128]{1,0:T(8,128)(2,1)S(1)} %select_convert_fusion.6), channel_id=1, source_target_pairs={{0,64},{8,72},{16,80},{24,88},{32,96},{40,104},{48,112},{56,120},{... | collective-permute-start | bytes 1056776 | tf_op jit(solution)/shard_map/ppermute | solution.py:42
  363.1 66.2 %collective-permute-start.107 = (bf16[688,1024]{1,0:T(8,128)(2,1)S(1)}, bf16[688,1024]{1,0:T(8,128)(2,1)S(1)}, u32[]{:S(2)}, u32[]{:S(2)}) collective-permute-start(bf16[688,1024]{1,0:T(8,128)(2,1)S(1)} %pad_maximum_fusion.4), channel_id=1, source_target_pairs={{0,8},{8,0},{16,24},{24,16},{32,40},{40,32},{48,56},{56,48},{64,72... | collective-permute-start | bytes 4227080 | tf_op jit(solution)/shard_map/ppermute | solution.py:42
  401.6 19.1 %collective-permute-start.94 = (bf16[1376,256]{1,0:T(8,128)(2,1)S(1)}, bf16[1376,256]{1,0:T(8,128)(2,1)S(1)}, u32[]{:S(2)}, u32[]{:S(2)}) collective-permute-start(bf16[1376,256]{1,0:T(8,128)(2,1)S(1)} %pad_maximum_fusion.6), channel_id=1, source_target_pairs={{0,48},{8,56},{16,32},{24,40},{32,16},{40,24},{48,0},{56,8},{64,11... | collective-permute-start | bytes 2113544 | tf_op jit(solution)/shard_map/ppermute | solution.py:42
  404.2 16.8 %collective-permute-start.92 = (bf16[1376,256]{1,0:T(8,128)(2,1)S(1)}, bf16[1376,256]{1,0:T(8,128)(2,1)S(1)}, u32[]{:S(2)}, u32[]{:S(2)}) collective-permute-start(bf16[1376,256]{1,0:T(8,128)(2,1)S(1)} %pad_maximum_fusion.5), channel_id=1, source_target_pairs={{0,16},{8,24},{16,0},{24,8},{32,48},{40,56},{48,32},{56,40},{64,80... | collective-permute-start | bytes 2113544 | tf_op jit(solution)/shard_map/ppermute | solution.py:42
  407.0 26.2 %collective-permute-start.83 = (bf16[1024,1024]{0,1:T(8,128)(2,1)S(1)}, bf16[1024,1024]{0,1:T(8,128)(2,1)S(1)}, u32[]{:S(2)}, u32[]{:S(2)}) collective-permute-start(bf16[1024,1024]{0,1:T(8,128)(2,1)S(1)} %pad_maximum_fusion.3), channel_id=1, source_target_pairs={{0,8},{8,0},{16,24},{24,16},{32,40},{40,32},{48,56},{56,48},{64,72... | collective-permute-start | bytes 6291464 | tf_op jit(solution)/shard_map/ppermute | solution.py:42
  423.3 22.3 %collective-permute-start.95 = (bf16[1376,1024]{1,0:T(8,128)(2,1)}, bf16[1376,1024]{1,0:T(8,128)(2,1)}, u32[]{:S(2)}, u32[]{:S(2)}) collective-permute-start(bf16[1376,1024]{1,0:T(8,128)(2,1)} %pad_maximum_fusion.1), channel_id=1, source_target_pairs={{0,8},{8,0},{16,24},{24,16},{32,40},{40,32},{48,56},{56,48},{64,72... | collective-permute-start | bytes 8454152 | tf_op jit(solution)/shard_map/ppermute | solution.py:42
  (135 other events, 1298.6 us)

commit v2 on v0

v2 whole, which is shorter than its diff:
```python
import jax
import jax.numpy as jnp
from jax import lax
from jax.experimental import pallas as pl
from jax.experimental.pallas import tpu as pltpu
from jax.sharding import Mesh
from jax.sharding import PartitionSpec as P

HD = 128
W = 1024
SEQ = 16
TP = 8
Z_FLIPS = (2, 1, 3)
FFN_PIECES = (
    ((0, 0, 688), (1, 0, 128)),
    ((1, 128, 688), (2, 0, 256)),
    ((2, 256, 688),),
)
FFN_ROWS = (816, 816, 432)

epsilon = 1e-06
masked_value = -1e30
low = jnp.bfloat16
wide = jnp.float32


def seq_pairs(step):
    pairs = []
    for x_hi in range(2):
        for y in range(4):
            for core in range(2):
                to = step(x_hi, y, core)
                if to is not None:
                    pairs.append((x_hi * 8 + y * 2 + core, to[0] * 8 + to[1] * 2 + to[2]))
    return pairs


EXCHANGE = {
    "core": seq_pairs(lambda x, y, c: (x, y, 1 - c)),
    "y1": seq_pairs(lambda x, y, c: (x, y ^ 1, c)),
    "y3": seq_pairs(lambda x, y, c: (x, y ^ 3, c)),
    "x": seq_pairs(lambda x, y, c: (1 - x, y, c)),
}

SEQ_AXES = ("x_hi", "y", "core")


def by_seq(value, name):
    return lax.ppermute(value, SEQ_AXES, EXCHANGE[name])


def by_tp(value, flip):
    return lax.ppermute(value, "tp", [(k, k ^ flip) for k in range(TP)])


def shifted(value, steps):
    pairs = [(k, k + steps) for k in range(SEQ) if 0 <= k + steps < SEQ]
    return lax.ppermute(value, SEQ_AXES, pairs)


def z_exchange(blocks):
    return [by_tp(block, 2 * flip) for flip, block in zip(Z_FLIPS, blocks)]


def z_spread(block):
    return [by_tp(block, 2 * flip) for flip in Z_FLIPS]


def places():
    x_hi = lax.axis_index("x_hi")
    y = lax.axis_index("y")
    core = lax.axis_index("core")
    tp = lax.axis_index("tp")
    return {
        "seq": x_hi * 8 + y * 2 + core,
        "tp": tp,
        "z": tp >> 1,
        "x_low": tp & 1,
        "core": core,
        "y1": (y & 1) ^ (y >> 1),
        "y3": y >> 1,
        "x": x_hi,
    }


class Order:
    def __init__(self):
        self.last = None

    def __call__(self, body, ins, outs, needs=(), scratch=(), temporary=2 << 20):
        ins = list(ins)
        needs = list(needs)
        if self.last is not None and not any(value is self.last for value in ins):
            needs.append(self.last)
        skip = len(ins) + len(needs)
        out_shape = [jax.ShapeDtypeStruct(shape, kind) for shape, kind in outs]
        count = len(ins)

        def run(*refs):
            body(refs[:count], refs[skip : skip + len(outs)], refs[skip + len(outs) :])

        def size(shape, kind):
            lanes = -(-shape[-1] // 128) * 128
            total = lanes * jnp.dtype(kind).itemsize
            for extent in shape[:-1]:
                total *= max(extent, 1)
            return total

        held = (
            sum(size(value.shape, value.dtype) for value in ins)
            + sum(size(shape, kind) for shape, kind in outs)
            + sum(size(shape, kind) for shape, kind in scratch)
        )
        result = pl.pallas_call(
            run,
            out_shape=out_shape,
            in_specs=[pl.BlockSpec(memory_space=pltpu.VMEM)] * count
            + [pl.BlockSpec(memory_space=pl.ANY)] * len(needs),
            out_specs=[pl.BlockSpec(memory_space=pltpu.VMEM)] * len(outs),
            scratch_shapes=[pltpu.VMEM(shape, kind) for shape, kind in scratch],
            compiler_params=pltpu.CompilerParams(vmem_limit_bytes=held + temporary),
            cost_estimate=pl.CostEstimate(flops=0, bytes_accessed=0, transcendentals=0),
            name=body.__name__,
        )(*ins, *needs)
        self.last = result[0]
        return result


def hold(order, values, needs=()):
    values = list(values)
    needs = list(needs) + [order.last]

    def run(*refs):
        pass

    return pl.pallas_call(
        run,
        out_shape=[jax.ShapeDtypeStruct(value.shape, value.dtype) for value in values],
        in_specs=[pl.BlockSpec(memory_space=pl.ANY)] * (len(values) + len(needs)),
        out_specs=[pl.BlockSpec(memory_space=pl.ANY)] * len(values),
        input_output_aliases={k: k for k in range(len(values))},
        compiler_params=pltpu.CompilerParams(vmem_limit_bytes=1 << 20),
        cost_estimate=pl.CostEstimate(flops=0, bytes_accessed=0, transcendentals=0),
    )(*values, *needs)


def dot(left, right):
    return jnp.dot(left, right, preferred_element_type=wide)


def dot_rows(left, right):
    return lax.dot_general(left, right, (((1,), (1,)), ((), ())), preferred_element_type=wide)


def dot_cols(left, right):
    return lax.dot_general(left, right, (((0,), (0,)), ((), ())), preferred_element_type=wide)


def rms_factor(rows):
    return lax.rsqrt(jnp.mean(rows * rows, axis=-1, keepdims=True) + epsilon)


def norm_back(grad_normed, unit_rows, factor, gain_vec):
    scaled = grad_normed * gain_vec
    return factor * (scaled - unit_rows * jnp.mean(scaled * unit_rows, axis=-1, keepdims=True))


def span(index, size):
    return pl.ds(pl.multiple_of(index * size, size), size)


def write_blocks(partial, z, outs):
    size = outs[0].shape[0]
    for flip, out in zip((0,) + Z_FLIPS, outs):
        out[...] = partial[span(z ^ flip, size), :]


def read_blocks(whole, z, blocks, first=0, width=None):
    size = blocks[0].shape[0]
    for flip, block in zip((0,) + Z_FLIPS, blocks):
        value = block[...] if width is None else block[:, first : first + width]
        whole[span(z ^ flip, size), :] = value.astype(whole.dtype)


def normed_kernel(ins, outs, _):
    tokens, gain, w_key, w_value = ins
    normed, key_value = outs
    inputs = tokens[...].astype(wide)
    rows = (inputs * rms_factor(inputs) * gain[...]).astype(low)
    normed[...] = rows
    features = w_key.shape[1]
    key_value[:, :features] = dot(rows, w_key[...]).astype(low)
    key_value[:, features:] = dot(rows, w_value[...]).astype(low)


def project_kernel(ins, outs, _):
    outs[0][...] = dot(ins[0][...], ins[1][...]).astype(low)


def last_block(at, own_of_partner, four_of_partner, way):
    near = at["core"] == (0 if way == 1 else 1)
    return jnp.where(near, four_of_partner, own_of_partner)


def seen_scores(scores, order, distance, gap, inside):
    if order == 0:
        return jnp.where(gap >= 0, scores, masked_value)
    if order == 3:
        return jnp.where((gap < 0) & inside, scores, masked_value)
    return jnp.where(inside, scores, masked_value)


def distances(at, way):
    near = at["core"] == (0 if way == 1 else 1)
    return [0, 2, jnp.where(near, 1, 3), 4, jnp.where(near, 3, 1)]


def gap_of(rows, flipped=False):
    first = lax.broadcasted_iota(jnp.int32, (rows, rows), 0)
    second = lax.broadcasted_iota(jnp.int32, (rows, rows), 1)
    return second - first if flipped else first - second


def attend_kernel(ins, outs, scratch):
    query, own, two, across, four, partner_own, partner_four, w_out = ins
    side, log_out = outs[:2]
    rows, features = query.shape
    at = places()
    scale = HD ** (-0.5)
    gap = gap_of(rows)
    away = distances(at, 1)
    blocks = [own[...], two[...], across[...], four[...]]
    blocks.append(last_block(at, partner_own[...], partner_four[...], 1))
    logs = []
    mixed = []
    for head in range(features // HD):
        here = slice(head * HD, (head + 1) * HD)
        there = slice(features + head * HD, features + (head + 1) * HD)
        scores = [
            seen_scores(
                dot_rows(query[:, here], block[:, here]) * scale,
                order,
                distance,
                gap,
                at["seq"] >= distance,
            )
            for order, (block, distance) in enumerate(zip(blocks, away))
        ]
        peak = scores[0].max(axis=-1, keepdims=True)
        for part in scores[1:]:
            peak = jnp.maximum(peak, part.max(axis=-1, keepdims=True))
        raised = [jnp.exp(part - peak) for part in scores]
        total = raised[0].sum(axis=-1, keepdims=True)
        for part in raised[1:]:
            total = total + part.sum(axis=-1, keepdims=True)
        inverse = 1.0 / total
        out = dot((raised[0] * inverse).astype(low), blocks[0][:, there])
        for part, block in zip(raised[1:], blocks[1:]):
            out = out + dot((part * inverse).astype(low), block[:, there])
        mixed.append(out.astype(low))
        logs.append(peak + jnp.log(total))
    lane = lax.broadcasted_iota(jnp.int32, (rows, HD), 1)
    both = jnp.where((lane & 32) == 0, logs[0], logs[1])
    first = both.astype(low).astype(wide)
    side[:, :features] = query[...]
    for head, out in enumerate(mixed):
        side[:, features + head * HD : features + (head + 1) * HD] = out
    side[:, 2 * features :] = jnp.where(lane < 64, first, both - first).astype(low)
    log_out[...] = jnp.where(lane < 64, logs[0], logs[1])
    partial = scratch[0]
    partial[...] = dot(side[:, features : 2 * features], w_out[...]).astype(low)
    write_blocks(partial, at["z"], outs[2:])


def sum_z_kernel(ins, outs, _):
    keep, send = outs
    at = places()
    size, width = keep.shape[0], ins[0].shape[1]
    for group in range(len(ins) // 4):
        blocks = ins[4 * group : 4 * group + 4]
        here = slice(group * width, (group + 1) * width)
        for out, index in ((keep, at["x_low"]), (send, 1 - at["x_low"])):
            total = blocks[0][span(index, size), :].astype(wide)
            for block in blocks[1:]:
                total = total + block[span(index, size), :].astype(wide)
            out[:, here] = total.astype(out.dtype)


def norm_rows_kernel(ins, outs, _):
    keep, arrived, tokens, gain = ins
    hidden, normed = outs
    at = places()
    rows = tokens[span(at["tp"], keep.shape[0]), :].astype(wide) + (
        keep[...] + arrived[...].astype(wide)
    )
    hidden[...] = rows
    normed[...] = (rows * rms_factor(rows) * gain[...]).astype(low)


def pair_kernel(ins, outs, _):
    at = places()
    size = ins[0].shape[0]
    outs[0][span(at["x_low"], size), :] = ins[0][...]
    outs[0][span(1 - at["x_low"], size), :] = ins[1][...]


def ffn_kernel(ins, outs, scratch):
    pair, block_two, block_one, block_three, w_gate, w_up, w_down, cotangent = ins
    normed, activated, grad_gate, grad_up = outs[:4]
    at = places()
    read_blocks(normed, at["z"], (pair, block_two, block_one, block_three))
    rows = normed[...]
    gate_pre = dot_rows(rows, w_gate[...])
    up_pre = dot_rows(rows, w_up[...])
    grad_act = dot_rows(cotangent[...], w_down[...])
    sigmoid = jax.nn.sigmoid(gate_pre)
    silu = gate_pre * sigmoid
    activated[...] = (silu * up_pre).astype(low)
    grad_gate[...] = (grad_act * up_pre * sigmoid * (1.0 + gate_pre * (1.0 - sigmoid))).astype(low)
    grad_up[...] = (grad_act * silu).astype(low)
    partial = scratch[0]
    partial[...] = (dot(grad_gate[...], w_gate[...]) + dot(grad_up[...], w_up[...])).astype(low)
    write_blocks(partial, at["z"], outs[4:])


def grad_rows_kernel(ins, outs, _):
    keep, arrived, hidden, cotangent, gain = ins
    grad_hidden, grad_low, gain_part = outs
    at = places()
    grad_normed = keep[...] + arrived[...].astype(wide)
    rows = hidden[...]
    factor = rms_factor(rows)
    unit = rows * factor
    gain_part[...] = jnp.sum(grad_normed * unit, axis=0, keepdims=True)
    grad = cotangent[span(at["tp"], keep.shape[0]), :].astype(wide) + norm_back(
        grad_normed, unit, factor, gain[...]
    )
    grad_hidden[...] = grad
    grad_low[...] = grad.astype(low)


def heads_kernel(ins, outs, _):
    grad_hidden, grad_heads = outs
    read_blocks(grad_hidden, places()["z"], ins[:4])
    grad_heads[...] = dot_rows(grad_hidden[...], ins[4][...]).astype(low)


def grad_query_kernel(ins, outs, _):
    side, logs, grad_heads, own, two, across, four, partner_own, partner_four = ins
    rows, features = grad_heads.shape
    at = places()
    scale = HD ** (-0.5)
    gap = gap_of(rows)
    away = distances(at, 1)
    blocks = [own[...], two[...], across[...], four[...]]
    blocks.append(last_block(at, partner_own[...], partner_four[...], 1))
    for head in range(features // HD):
        here = slice(head * HD, (head + 1) * HD)
        there = slice(features + head * HD, features + (head + 1) * HD)
        query = side[:, here]
        grad = grad_heads[:, here]
        log_total = logs[:, head * 64 : head * 64 + 1]
        inner = jnp.sum(
            grad.astype(wide) * side[:, there].astype(wide), axis=-1, keepdims=True
        )
        total = jnp.zeros((rows, HD), wide)
        for order, (block, distance) in enumerate(zip(blocks, away)):
            scores = seen_scores(
                dot_rows(query, block[:, here]) * scale,
                order,
                distance,
                gap,
                at["seq"] >= distance,
            )
            weights = jnp.exp(scores - log_total)
            grad_scores = weights * (dot_rows(grad, block[:, there]) - inner)
            total = total + dot(grad_scores.astype(low), block[:, here])
        outs[0][:, here] = (total * scale).astype(low)


def grad_key_kernel(ins, outs, scratch):
    key_value = ins[0]
    sides = ins[1:7]
    grads = ins[7:13]
    grad_query, w_query, w_key, w_value, tokens, gain_ffn_part, ffn_partial = ins[13:]
    grad_key, grad_value, keep_one, keep_two, send_one, send_two = outs
    rows, features = grad_query.shape
    at = places()
    scale = HD ** (-0.5)
    gap = gap_of(rows, flipped=True)
    away = distances(at, -1)
    side_blocks = [side[...] for side in sides[:4]]
    side_blocks.append(last_block(at, sides[4][...], sides[5][...], -1))
    grad_blocks = [grad[...] for grad in grads[:4]]
    grad_blocks.append(last_block(at, grads[4][...], grads[5][...], -1))
    log_rows = [side[:, 2 * features :].astype(wide).T for side in side_blocks]
    for head in range(features // HD):
        here = slice(head * HD, (head + 1) * HD)
        there = slice(features + head * HD, features + (head + 1) * HD)
        key = key_value[:, here]
        value = key_value[:, there]
        total_key = jnp.zeros((rows, HD), wide)
        total_value = jnp.zeros((rows, HD), wide)
        for order, (side, grad_all, logs, distance) in enumerate(
            zip(side_blocks, grad_blocks, log_rows, away)
        ):
            query = side[:, here]
            grad = grad_all[:, here]
            log_total = logs[head * 32 : head * 32 + 1] + logs[64 + head * 32 : 65 + head * 32]
            inner = jnp.sum(
                (grad.astype(wide) * side[:, there].astype(wide)).T, axis=0, keepdims=True
            )
            scores = seen_scores(
                dot_rows(key, query) * scale, order, distance, gap, at["seq"] + distance < SEQ
            )
            weights = jnp.exp(scores - log_total)
            total_value = total_value + dot(weights.astype(low), grad)
            grad_scores = weights * (dot_rows(value, grad) - inner)
            total_key = total_key + dot(grad_scores.astype(low), query)
        grad_key[:, here] = (total_key * scale).astype(low)
        grad_value[:, here] = total_value.astype(low)
    back = (
        dot_rows(grad_query[...], w_query[...])
        + dot_rows(grad_key[...], w_key[...])
        + dot_rows(grad_value[...], w_value[...])
    )
    inputs = tokens[...].astype(wide)
    gain_attn_part = jnp.sum(back * (inputs * rms_factor(inputs)), axis=0, keepdims=True)
    partial = scratch[0]
    width = tokens.shape[1]
    partial[:, :width] = back.astype(low)
    share = rows // TP
    cells = width // TP // HD
    for k in range(TP):
        parts = [
            gain[:, (k * cells + cell) * HD : (k * cells + cell + 1) * HD]
            for gain in (gain_attn_part, gain_ffn_part[...])
            for cell in range(cells)
        ]
        parts.append(jnp.zeros((share - len(parts), HD), wide))
        partial[k * share : (k + 1) * share, width:] = jnp.concatenate(parts, axis=0).astype(low)
    size = rows // 4
    z = at["z"]
    cut = width // 2
    for out, first, flips in (
        (keep_one, 0, (0, 3)),
        (send_one, 0, (1, 2)),
        (keep_two, cut, (0, 1)),
        (send_two, cut, (3, 2)),
    ):
        for k, flip in enumerate(flips):
            here = slice(k * size, (k + 1) * size)
            there = span(z ^ flip, size)
            out[here, :cut] = partial[there, first : first + cut]
            out[here, cut:width] = ffn_partial[there, first : first + cut]
            if first > 0:
                out[here, width:] = partial[there, width:]


def sum_middle_kernel(ins, outs, _):
    for keep, arrived, stay, send in ((ins[0], ins[1], outs[0], outs[1]), (ins[2], ins[3], outs[2], outs[3])):
        size = stay.shape[0]
        stay[...] = keep[:size, :].astype(wide) + arrived[:size, :].astype(wide)
        send[...] = (keep[size:, :].astype(wide) + arrived[size:, :].astype(wide)).astype(low)


def sum_last_kernel(ins, outs, _):
    keep, send = outs
    at = places()
    size = keep.shape[0]
    width = ins[0].shape[1]
    cut = width // 2
    for out, index in ((keep, at["x_low"]), (send, 1 - at["x_low"])):
        here = span(index, size)
        first = (ins[0][here, :] + ins[1][here, :].astype(wide)).astype(out.dtype)
        second = (ins[2][here, :] + ins[3][here, :].astype(wide)).astype(out.dtype)
        out[:, :cut] = first[:, :cut]
        out[:, cut:width] = second[:, :cut]
        out[:, width : width + cut] = first[:, cut:]
        out[:, width + cut : 2 * width] = second[:, cut:width]
        out[:, 2 * width :] = second[:, width:]


def last_rows_kernel(ins, outs, _):
    keep, arrived, grad_hidden, hidden, tokens, gain = ins
    rows_out, gains = outs
    width = hidden.shape[1]
    at = places()
    inputs = tokens[span(at["tp"], keep.shape[0]), :].astype(wide)
    factor = rms_factor(inputs)
    grad_normed = keep[:, :width] + arrived[:, :width].astype(wide)
    grad = grad_hidden[...] + norm_back(grad_normed, inputs * factor, factor, gain[...])
    rows_out[:, :width] = grad.astype(low)
    rows_out[:, width:] = (
        hidden[...] + keep[:, width : 2 * width] + arrived[:, width : 2 * width].astype(wide)
    ).astype(low)
    sums = keep[:, 2 * width :] + arrived[:, 2 * width :].astype(wide)
    gains[...] = jnp.zeros_like(gains)
    gains[:, : sums.shape[1]] = sums[: gains.shape[0], :].astype(low)


def last_pair_kernel(ins, outs, _):
    at = places()
    size = ins[0].shape[0]
    width = outs[0].shape[1]
    for value, index in zip(ins, (at["x_low"], 1 - at["x_low"])):
        outs[0][span(index, size), :] = value[:, :width]
        outs[1][span(index, size), :] = value[:, width:]


def stack_kernel(ins, outs, _):
    for k, out in enumerate(outs):
        size = ins[2 * k].shape[0]
        out[:size, :] = ins[2 * k][...]
        out[size:, :] = ins[2 * k + 1][...]


def token_outputs_kernel(ins, outs, _):
    z = places()["z"]
    size = ins[0].shape[0] // 2
    for out, own, arrived, flips in (
        (outs[0], ins[0], ins[1], (0, 1, 3, 2)),
        (outs[1], ins[2], ins[3], (0, 3, 1, 2)),
    ):
        blocks = (own[:size, :], own[size:, :], arrived[:size, :], arrived[size:, :])
        for flip, block in zip(flips, blocks):
            out[span(z ^ flip, size), :] = block.astype(out.dtype)


def part(ref, axis, start, size):
    return ref[:, pl.ds(start, size)] if axis == 1 else ref[pl.ds(start, size), :]


def put(ref, axis, start, size, value):
    if axis == 1:
        ref[:, pl.ds(start, size)] = value
    else:
        ref[pl.ds(start, size), :] = value


def split_op(keep, arrived, bit, axis):
    shape = list(keep.shape)
    shape[axis] //= 2
    size = shape[axis]

    def body(at, ins, outs):
        for out, index in zip(outs, (at[bit], 1 - at[bit])):
            start = pl.multiple_of(index * size, size)
            out[...] = (
                part(ins[0], axis, start, size).astype(wide)
                + part(ins[1], axis, start, size).astype(wide)
            ).astype(low)

    return body, [keep, arrived], [(tuple(shape), low)] * 2


def add_op(keep, arrived):
    def body(at, ins, outs):
        outs[0][...] = (ins[0][...].astype(wide) + ins[1][...].astype(wide)).astype(
            outs[0].dtype
        )

    return body, [keep, arrived], [(keep.shape, keep.dtype)]


def join_op(own, arrived, bit, axis, kind=low):
    shape = list(own.shape)
    size = shape[axis]
    shape[axis] *= 2

    def body(at, ins, outs):
        for value, index in zip(ins, (at[bit], 1 - at[bit])):
            start = pl.multiple_of(index * size, size)
            put(outs[0], axis, start, size, value[...].astype(kind))

    return body, [own, arrived], [(tuple(shape), kind)]


def add_tail_op(keep, arrived, tail):
    rows, width = keep.shape

    def body(at, ins, outs):
        outs[0][:rows, :] = (ins[0][...].astype(wide) + ins[1][...].astype(wide)).astype(low)
        outs[0][rows:, :] = ins[2][...]

    return body, [keep, arrived, tail], [((rows + tail.shape[0], width), low)]


def join_tail_op(own, arrived, bit, tail):
    rows, width = own.shape
    size = rows - tail

    def body(at, ins, outs):
        for value, index in zip(ins, (at[bit], 1 - at[bit])):
            outs[0][span(index, size), :] = value[:size, :]
        outs[0][2 * size :, :] = (
            ins[0][size:, :].astype(wide) + ins[1][size:, :].astype(wide)
        ).astype(low)

    return body, [own, arrived], [((2 * size + tail, width), low)]


def run_ops(order, ops, needs=()):
    ins = [value for _, values, _ in ops for value in values]
    outs = [out for _, _, shapes in ops for out in shapes]

    def body(in_refs, out_refs, _):
        at = places()
        first = last = 0
        for step, values, shapes in ops:
            step(
                at,
                in_refs[first : first + len(values)],
                out_refs[last : last + len(shapes)],
            )
            first += len(values)
            last += len(shapes)

    flat = list(order(body, ins, outs, needs))
    result = []
    for _, _, shapes in ops:
        result.append(flat[: len(shapes)])
        flat = flat[len(shapes) :]
    return result


FFN_ORDERS = (("y1", "y3", "x"), ("y3", "x", "y1"), ("x", "y1", "y3"))


def ffn_terms(ins, k):
    terms = []
    first = 0
    for operand, start, stop in FFN_PIECES[k]:
        last = first + stop - start
        terms.append((first, last, ins[operand][:, start:stop], ins[4 if operand == 2 else 3]))
        first = last
    return terms


def ffn_send_kernel(arrays):
    def ffn_send(ins, outs, _):
        out = outs[0]
        half = out.shape[1]
        other = 1 - places()["core"]
        base = 0
        for k in arrays:
            for first, last, left, right in ffn_terms(ins, k):
                out[base + first : base + last, :] = dot_cols(
                    left, right[:, span(other, half)]
                ).astype(low)
            base += FFN_ROWS[k]

    return ffn_send


def ffn_keep_kernel(arrays):
    def ffn_keep(ins, outs, _):
        at = places()
        arrived = ins[5]
        base = 0
        for k, keep, send in zip(arrays, outs[0::2], outs[1::2]):
            size = keep.shape[1]
            bit = at[FFN_ORDERS[k][0]]
            for out, index in ((keep, bit), (send, 1 - bit)):
                start = pl.multiple_of((2 * at["core"] + index) * size, size)
                for first, last, left, right in ffn_terms(ins, k):
                    own = dot_cols(left, right[:, pl.ds(start, size)])
                    got = arrived[base + first : base + last, span(index, size)]
                    out[first:last, :] = (own + got.astype(wide)).astype(low)
            base += FFN_ROWS[k]

    return ffn_keep


def attn_terms(ins):
    normed, grad_hidden, grad_query, grad_key, grad_value, heads_out = ins
    half = heads_out.shape[1] // 2
    return [
        [(normed, grad_query[...]), (grad_hidden, heads_out[:, :half])],
        [(normed, grad_key[...]), (grad_hidden, heads_out[:, half:])],
        [(normed, grad_value[...])],
    ]


def attn_send_kernel(ins, outs, _):
    out = outs[0]
    half = out.shape[0]
    other = 1 - places()["core"]
    first = 0
    for terms in attn_terms(ins):
        for left, right in terms:
            last = first + right.shape[1]
            out[:, first:last] = dot_cols(left[:, span(other, half)], right).astype(low)
            first = last


ATTN_ORDERS = (("y1", "y3", "x"), ("y3", "x", "y1"), ("x", "y1", "y3"))


def packed_rows(rows, lanes, width):
    across = width // 128
    full, rest = divmod(lanes // 128, across)
    if rest == 1 and rows % across == 0:
        return rows * full + rows // across
    return rows * (full + (rest > 0))


def place_cells(rows, lanes, width):
    across = width // 128
    cells = lanes // 128
    runs = []
    full = cells // across
    for k in range(full * across):
        runs.append((0, k * 128, (k // across) * rows, (k % across) * 128, rows))
    rest = cells - full * across
    if rest and rows % across == 0 and rest == 1:
        size = rows // across
        for k in range(across):
            runs.append((k * size, full * across * 128, full * rows, k * 128, size))
    elif rest:
        for k in range(rest):
            runs.append((0, (full * across + k) * 128, full * rows, k * 128, rows))
    return runs


def pack(message, base, value):
    rows, lanes = value.shape
    for row, lane, to_row, to_lane, size in place_cells(rows, lanes, message.shape[1]):
        message[base + to_row : base + to_row + size, to_lane : to_lane + 128] = value[
            row : row + size, lane : lane + 128
        ]


def add_packed(keep, message, base, lanes):
    rows = keep.shape[0]
    columns = [[] for _ in range(lanes // 128)]
    for row, lane, from_row, from_lane, size in place_cells(rows, lanes, message.shape[1]):
        here = keep[row : row + size, lane : lane + 128].astype(wide)
        there = message[base + from_row : base + from_row + size, from_lane : from_lane + 128]
        columns[lane // 128].append(here + there.astype(wide))
    return [jnp.concatenate(parts, axis=0) if len(parts) > 1 else parts[0] for parts in columns]


ATTN_ORDERS = (("y1", "y3", "x"), ("y3", "x", "y1"), ("x", "y1", "y3"))
WAYS = ("y1", "y3", "x")


def round_one_kernel(ins, outs, _):
    at = places()
    operands, arrived = ins[6:12], ins[12]
    messages = dict(zip(WAYS, outs[:3]))
    tops = {orders[2]: rows for orders, rows in zip(FFN_ORDERS, FFN_ROWS)}
    for k in range(3):
        messages[FFN_ORDERS[k][2]][: FFN_ROWS[k], :] = (
            ins[k][...].astype(wide) + ins[3 + k][...].astype(wide)
        ).astype(low)
    base = 0
    for k, terms in enumerate(attn_terms(operands)):
        keep = outs[3 + k]
        size, lanes = keep.shape
        way = ATTN_ORDERS[k][0]
        for kept, index in ((True, at[way]), (False, 1 - at[way])):
            start = pl.multiple_of((2 * at["core"] + index) * size, size)
            first = 0
            for left, right in terms:
                last = first + right.shape[1]
                value = dot_cols(left[:, pl.ds(start, size)], right)
                value = value + arrived[span(index, size), base + first : base + last].astype(wide)
                value = value.astype(low)
                if kept:
                    keep[:, first:last] = value
                else:
                    for lane in range(first, last, 128):
                        row = tops[way] + lane // 128 * size
                        messages[way][row : row + size, :] = value[
                            :, lane - first : lane - first + 128
                        ]
                first = last
        base += lanes


def round_next_kernel(step):
    def round_next(ins, outs, _):
        at = places()
        sent, arrived = dict(zip(WAYS, ins[:3])), dict(zip(WAYS, ins[3:6]))
        messages = dict(zip(WAYS, outs[:3]))
        came_tops = {orders[3 - step]: rows for orders, rows in zip(FFN_ORDERS, FFN_ROWS)}
        tops = {orders[2 - step]: rows for orders, rows in zip(FFN_ORDERS, FFN_ROWS)}
        for k in range(3):
            back = FFN_ORDERS[k][3 - step]
            message = messages[FFN_ORDERS[k][2 - step]]
            width = sent[back].shape[1]
            rows = FFN_ROWS[k]
            for value, index in ((sent[back], at[back]), (arrived[back], 1 - at[back])):
                start = pl.multiple_of(index * width, width)
                message[:rows, pl.ds(start, width)] = value[:rows, :]
        for k in range(3):
            keep = ins[6 + k]
            came, way = ATTN_ORDERS[k][step - 1], ATTN_ORDERS[k][step]
            columns = add_packed(keep, arrived[came], came_tops[came], keep.shape[1])
            size = keep.shape[0] // 2
            halves = []
            for column in columns:
                halves.append((column[:size, :], column[size:, :]))
            first = at[way] == 0
            stay = [jnp.where(first, one, two).astype(low) for one, two in halves]
            go = [jnp.where(first, two, one).astype(low) for one, two in halves]
            for lane, value in enumerate(stay):
                outs[3 + k][:, lane * 128 : (lane + 1) * 128] = value
            pack(messages[way], tops[way], jnp.concatenate(go, axis=1))

    return round_next


def round_last_kernel(ins, outs, _):
    arrived = dict(zip(WAYS, ins[:3]))
    tops = {orders[0]: rows for orders, rows in zip(FFN_ORDERS, FFN_ROWS)}
    for k in range(3):
        keep = ins[3 + k]
        rows = keep.shape[0]
        way = ATTN_ORDERS[k][2]
        columns = add_packed(keep, arrived[way], tops[way], keep.shape[1])
        for lane, column in enumerate(columns):
            outs[k][:rows, lane * 128 : (lane + 1) * 128] = column.astype(low)
    outs[2][ins[5].shape[0] :, :] = ins[6][...]


def ffn_halves_kernel(ins, outs, _):
    at = places()
    sent, arrived = dict(zip(WAYS, ins[:3])), dict(zip(WAYS, ins[3:]))
    base = 0
    for k, rows in enumerate(FFN_ROWS):
        way = FFN_ORDERS[k][0]
        width = sent[way].shape[1]
        for value, index in ((sent[way], at[way]), (arrived[way], 1 - at[way])):
            start = pl.multiple_of(index * width, width)
            outs[0][base : base + rows, pl.ds(start, width)] = value[:rows, :]
        base += rows


def attn_output_kernel(ins, outs, _):
    core = places()["core"]
    grad_query, grad_key, grad_value, grad_out, gain_attn, gain_ffn = outs
    features = grad_query.shape[1]
    half = ins[0].shape[0]
    for k in (0, 1):
        index = core if k == 0 else 1 - core
        one, two, three = ins[k], ins[2 + k], ins[4 + k]
        here = span(index, half)
        grad_query[here, :] = one[:, :features].astype(wide)
        grad_key[here, :] = two[:, :features].astype(wide)
        grad_value[here, :] = three[:half, :].astype(wide)
        grad_out[: features // 2, here] = one[:, features:].astype(wide).T
        grad_out[features // 2 :, here] = two[:, features:].astype(wide).T
    sums = ins[4][half:, :].astype(wide) + ins[5][half:, :].astype(wide)
    for k, out in enumerate((gain_attn, gain_ffn)):
        out[:, :HD] = sums[2 * k : 2 * k + 1, :HD]
        out[:, HD:] = sums[2 * k + 1 : 2 * k + 2, :HD]


def ffn_output(order, own, arrived, which, units):
    half = own.shape[1]

    def run(own_ref, arrived_ref, need_ref, out_ref):
        first = places()["core"] == 0
        one, two = own_ref[...].astype(wide), arrived_ref[...].astype(wide)
        out_ref[:, :half] = jnp.where(first, one, two)
        out_ref[:, half:] = jnp.where(first, two, one)

    result = pl.pallas_call(
        run,
        out_shape=jax.ShapeDtypeStruct((units, 2 * half), wide),
        grid=(1,),
        in_specs=[pl.BlockSpec((units, half), lambda k: (which, 0))] * 2
        + [pl.BlockSpec(memory_space=pl.ANY)],
        out_specs=pl.BlockSpec((units, 2 * half), lambda k: (0, 0)),
        compiler_params=pltpu.CompilerParams(vmem_limit_bytes=32 << 20),
        cost_estimate=pl.CostEstimate(flops=0, bytes_accessed=0, transcendentals=0),
    )(own, arrived, order.last)
    order.last = result
    return result


def on_device(
    tokens, gain_attn, w_query, w_key, w_value, w_out, gain_ffn, w_gate, w_up, w_down, cotangent
):
    rows, width = tokens.shape
    features = w_query.shape[1]
    units = w_gate.shape[1]
    share = rows // TP
    quarter = rows // 4
    order = Order()
    gain_attn = gain_attn.reshape(1, width)
    gain_ffn = gain_ffn.reshape(1, width)
    w_gate, w_up = w_gate.T, w_up.T
    blocks_out = [((quarter, width), low)] * 4
    whole = ((rows, width), low)
    small = ((rows, features), low)
    keep_and_send = [((share, width), wide), ((share, width), low)]

    normed_attn, own = order(
        normed_kernel,
        [tokens, gain_attn, w_key, w_value],
        [whole, ((rows, 2 * features), low)],
        temporary=6 << 20,
    )
    two, four = shifted(own, 2), shifted(own, 4)
    partner_own = by_seq(own, "core")
    (query,) = order(project_kernel, [normed_attn, w_query], [small])
    across = by_seq(two, "core")
    partner_four = by_seq(four, "core")
    keys = [own, two, across, four, partner_own, partner_four]
    side, logs, *blocks = order(
        attend_kernel,
        [query] + keys + [w_out],
        [((rows, 2 * features + HD), low), ((rows, HD), wide)] + blocks_out,
        scratch=[whole],
        temporary=6 << 20,
    )
    arrived = z_exchange(blocks[1:])
    keep, send = order(sum_z_kernel, [blocks[0]] + arrived, keep_and_send)
    arrived = by_tp(send, 1)

    hidden, normed_rows = order(norm_rows_kernel, [keep, arrived, tokens, gain_ffn], keep_and_send)
    arrived = by_tp(normed_rows, 1)

    (side_out,) = hold(order, [side])
    side_two, side_four = shifted(side_out, -2), shifted(side_out, -4)
    side_partner_own = by_seq(side_out, "core")

    (pair,) = order(pair_kernel, [normed_rows, arrived], [((quarter, width), low)])
    arrived = z_spread(pair)

    normed_ffn, activated, grad_gate, grad_up, *blocks = order(
        ffn_kernel,
        [pair] + arrived + [w_gate, w_up, w_down, cotangent],
        [whole] + [((rows, units), low)] * 3 + blocks_out,
        needs=[side_two, side_four],
        scratch=[whole],
        temporary=12 << 20,
    )
    side_across = by_seq(side_two, "core")
    side_partner_four = by_seq(side_four, "core")
    arrived = z_exchange(blocks[1:])
    ffn_operands = [grad_gate, grad_up, activated, normed_ffn, cotangent]
    half = width // 2
    (sent,) = order(ffn_send_kernel([2]), ffn_operands, [((FFN_ROWS[2], half), low)])
    last_arrived = by_seq(sent, "core")
    (sent,) = order(
        ffn_send_kernel([0, 1]),
        ffn_operands,
        [((FFN_ROWS[0] + FFN_ROWS[1], half), low)],
        needs=[side_across, side_partner_own, side_partner_four],
        temporary=5 << 20,
    )
    first_arrived = by_seq(sent, "core")
    last_keep, last_send = order(
        ffn_keep_kernel([2]),
        ffn_operands + [last_arrived],
        [((FFN_ROWS[2], half // 2), low)] * 2,
    )
    last_arrived = by_seq(last_send, FFN_ORDERS[2][0])
    parts = order(
        ffn_keep_kernel([0, 1]),
        ffn_operands + [first_arrived],
        [((FFN_ROWS[k], half // 2), low) for k in (0, 0, 1, 1)],
        temporary=5 << 20,
    )
    ffn_keeps = [parts[0], parts[2], last_keep]
    ffn_flights = [by_seq(parts[1 + 2 * k], FFN_ORDERS[k][0]) for k in (0, 1)] + [last_arrived]

    def ffn_split(step):
        nonlocal ffn_keeps, ffn_flights
        parts = run_ops(
            order,
            [
                split_op(keep, got, names[step], 1)
                for keep, got, names in zip(ffn_keeps, ffn_flights, FFN_ORDERS)
            ],
        )
        ffn_keeps = [keep for keep, _ in parts]
        ffn_flights = [by_seq(send, names[step]) for (_, send), names in zip(parts, FFN_ORDERS)]

    keep, send = order(sum_z_kernel, [blocks[0]] + arrived, keep_and_send)
    arrived = by_tp(send, 1)
    grad_hidden, grad_low, gain_ffn_part = order(
        grad_rows_kernel,
        [keep, arrived, hidden, cotangent, gain_ffn],
        keep_and_send + [((1, width), wide)],
    )
    arrived = by_tp(grad_low, 1)
    (pair,) = order(pair_kernel, [grad_low, arrived], [((quarter, width), low)])
    arrived = z_spread(pair)
    ffn_split(1)

    grad_hidden_low, grad_heads = order(heads_kernel, [pair] + arrived + [w_out], [whole, small])
    grad_two, grad_four = shifted(grad_heads, -2), shifted(grad_heads, -4)
    grad_partner_own = by_seq(grad_heads, "core")
    (grad_query,) = order(
        grad_query_kernel, [side_out, logs, grad_heads] + keys, [small], temporary=6 << 20
    )
    (ffn_partial,) = order(project_kernel, [activated, w_down], [whole], temporary=6 << 20)
    ffn_split(2)
    grad_two, grad_four = hold(order, [grad_two, grad_four])
    grad_across = by_seq(grad_two, "core")
    grad_partner_four = by_seq(grad_four, "core")
    cut = width
    grad_key, grad_value, keep_one, keep_two, send_one, send_two = order(
        grad_key_kernel,
        [own, side_out, side_two, side_across, side_four, side_partner_own, side_partner_four]
        + [grad_heads, grad_two, grad_across, grad_four, grad_partner_own, grad_partner_four]
        + [grad_query, w_query, w_key, w_value, tokens, gain_ffn_part, ffn_partial],
        [small, small] + [((2 * quarter, cut), low), ((2 * quarter, cut + HD), low)] * 2,
        needs=ffn_flights,
        scratch=[((rows, width + HD), low)],
        temporary=12 << 20,
    )
    one_arrived, two_arrived = by_tp(send_one, 2), by_tp(send_two, 6)

    heads_out = side_out[:, features : 2 * features]
    operands = [normed_attn, grad_hidden_low, grad_query, grad_key, grad_value, heads_out]
    (sent,) = order(
        attn_send_kernel, operands, [((width // 2, 4 * features), low)], temporary=4 << 20
    )
    core_arrived = by_seq(sent, "core")
    widths = (features + features // 2, features + features // 2, features)

    def round_shapes(step):
        lanes = 128 << step
        size = width // 4 >> step
        by_way = {orders[step]: part for orders, part in zip(ATTN_ORDERS, widths)}
        tops = {orders[2 - step]: part for orders, part in zip(FFN_ORDERS, FFN_ROWS)}
        messages = [
            ((tops[way] + packed_rows(size, by_way[way], lanes), lanes), low) for way in WAYS
        ]
        return messages + [((size, lanes_attn), low) for lanes_attn in widths]

    def fly(messages):
        return [by_seq(message, way) for message, way in zip(messages, WAYS)]

    *parts, keep_x, keep_y, keep_z = order(
        round_one_kernel,
        list(ffn_keeps) + ffn_flights + operands + [core_arrived],
        round_shapes(0),
        temporary=4 << 20,
    )
    flights = fly(parts)

    stay_one, go_one, stay_two, go_two = order(
        sum_middle_kernel,
        [keep_one, one_arrived, keep_two, two_arrived],
        [
            ((quarter, cut), wide),
            ((quarter, cut), low),
            ((quarter, cut + HD), wide),
            ((quarter, cut + HD), low),
        ],
    )
    one_arrived, two_arrived = by_tp(go_one, 6), by_tp(go_two, 2)

    *parts, keep_x, keep_y, keep_z = order(
        round_next_kernel(1), parts + flights + [keep_x, keep_y, keep_z], round_shapes(1)
    )
    flights = fly(parts)
    keep, send = order(
        sum_last_kernel,
        [stay_one, one_arrived, stay_two, two_arrived],
        [((share, 2 * width + HD), wide), ((share, 2 * width + HD), low)],
    )
    arrived = by_tp(send, 1)
    last_rows, gains = order(
        last_rows_kernel,
        [keep, arrived, grad_hidden, hidden, tokens, gain_attn],
        [((share, 2 * width), low), ((16, features), low)],
    )
    arrived = by_tp(last_rows, 1)
    *parts, keep_x, keep_y, keep_z = order(
        round_next_kernel(2), parts + flights + [keep_x, keep_y, keep_z], round_shapes(2)
    )
    flights = fly(parts)
    first, second = order(last_pair_kernel, [last_rows, arrived], [((quarter, width), low)] * 2)
    first_arrived, second_arrived = by_tp(first, 2), by_tp(second, 6)
    firsts, seconds = order(
        stack_kernel,
        [first, first_arrived, second, second_arrived],
        [((2 * quarter, width), low)] * 2,
    )
    first_arrived, second_arrived = by_tp(firsts, 6), by_tp(seconds, 2)

    one, two, three = order(
        round_last_kernel,
        flights + [keep_x, keep_y, keep_z, gains],
        [((128, widths[0]), low), ((128, widths[1]), low), ((128 + 16, widths[2]), low)],
    )
    (ffn_half,) = order(ffn_halves_kernel, parts + flights, [((3 * units, width // 2), low)])
    flights = [by_seq(one, "x"), by_seq(two, "y1"), by_seq(three, "y3")]
    ffn_arrived = by_seq(ffn_half, "core")

    def attn_join(step):
        nonlocal one, two, three, flights
        names = [orders[step] for orders in ATTN_ORDERS]
        (one,), (two,), (three,) = run_ops(
            order,
            [
                join_op(one, flights[0], names[0], 0),
                join_op(two, flights[1], names[1], 0),
                join_tail_op(three, flights[2], names[2], gains.shape[0]),
            ],
        )
        names = [orders[step - 1] if step > 0 else "core" for orders in ATTN_ORDERS]
        flights = [by_seq(value, name) for value, name in zip((one, two, three), names)]

    attn_join(2)
    grad_tokens, block_out = order(
        token_outputs_kernel,
        [firsts, first_arrived, seconds, second_arrived],
        [((rows, width), wide), whole],
    )
    attn_join(1)
    grads_ffn = [ffn_output(order, ffn_half, ffn_arrived, k, units) for k in range(3)]
    attn_join(0)
    grad_w_query, grad_w_key, grad_w_value, grad_w_out, grad_gain_attn, grad_gain_ffn = order(
        attn_output_kernel,
        [one, flights[0], two, flights[1], three, flights[2]],
        [((width, features), wide)] * 3 + [((features, width), wide)] + [((1, features), wide)] * 2,
    )
    return (
        block_out,
        grad_tokens,
        grad_gain_attn.reshape(-1),
        grad_w_query,
        grad_w_key,
        grad_w_value,
        grad_w_out,
        grad_gain_ffn.reshape(-1),
        grads_ffn[0].T,
        grads_ffn[1].T,
        grads_ffn[2],
    )


def solution(mesh):
    fine = Mesh(mesh.devices.reshape(2, 4, 2, TP), SEQ_AXES + ("tp",))
    return jax.shard_map(
        on_device,
        mesh=fine,
        in_specs=(
            P(SEQ_AXES, None),
            P(),
            P(None, "tp"),
            P(None, "tp"),
            P(None, "tp"),
            P("tp", None),
            P(),
            P(None, "tp"),
            P(None, "tp"),
            P("tp", None),
            P(SEQ_AXES, None),
        ),
        out_specs=(
            P(SEQ_AXES, None),
            P(SEQ_AXES, None),
            P("tp"),
            P(None, "tp"),
            P(None, "tp"),
            P(None, "tp"),
            P("tp", None),
            P("tp"),
            P(None, "tp"),
            P(None, "tp"),
            P("tp", None),
        ),
        check_vma=False,
    )
```

time: 650 us -> 316 us (0.49)
  waiting for transfers between devices: 456 us -> 137 us
  starting transfers between devices: 47.9 us -> 118 us
  matrix products: 42 us -> 0 us
  Pallas kernels: 0 us -> 39.9 us
  other arithmetic: 36.7 us -> 0 us
  blocking collectives: 33.5 us -> 0 us
  between operations: 14.5 us -> 1.45 us
    psum x4 -> x0, waiting for transfers between devices: 442 us -> none  [the longest x1 138 us: on_device(): lax.psum(grad_w_query.astype(jnp.bfloat16), 'seq').astype(jnp.float32)]
    ppermute x16 -> x75, waiting for transfers between devices: 13.8 us -> 137 us  [the longest x26 101 us: by_tp(): return lax.ppermute(value, 'tp', [(k, k ^ flip) for k in range(TP)])]
    ppermute x16 -> x75, starting transfers between devices: 47.4 us -> 118 us  [the longest x43 75 us: by_seq(): return lax.ppermute(value, SEQ_AXES, EXCHANGE[name])]
    dot_general x27 -> x0, matrix products: 42 us -> none  [the longest x7 13.6 us: outer_sum(): lax.dot_general(left_matrix, right_matrix, (((0,), (0,)), ((), ())), pref...]
    pallas_call x0 -> x41, Pallas kernels: none -> 39.9 us  [the longest x36 30.3 us: __call__(): pl.pallas_call(run, out_shape=out_shape, in_specs=[pl.BlockSpec(memory_sp...]
    psum x1 -> x0, blocking collectives: 33.5 us -> none  [on_device(): lax.psum(grad_gain_attn.astype(jnp.bfloat16), 'seq').astype(jnp.float32)]
    convert_element_type x14 -> x0, other arithmetic: 21.8 us -> none  [the longest x1 3.25 us: on_device(): lax.psum(grad_w_up.astype(jnp.bfloat16), 'seq').astype(jnp.float32)]
    reduce_sum x5 -> x0, other arithmetic: 9.74 us -> none  [the longest x2 3.87 us: rms_factor(): jnp.mean(field_rows * field_rows, axis=-1, keepdims=True) + epsilon]
  transfers between devices with their start and end apart: 20 -> 75, of which waited for: 11 -> 31; matrix products, arithmetic and copies ran while one was open for 5% -> 0% of each run, Pallas kernels for 0% -> 8%
where the time goes in v2:
time: 316 us; the launch traced here: 310 us
  waiting for transfers between devices  137 us (43%)
  starting transfers between devices  118 us (37%)
  Pallas kernels  39.9 us (13%)
  local copies, waits for them, and re-layouts  13.8 us (4%)
    ppermute x26, waiting for transfers between devices, by_tp(): return lax.ppermute(value, 'tp', [(k, k ^ flip) for k in range(TP)])  101 us
    ppermute x43, starting transfers between devices, by_seq(): return lax.ppermute(value, SEQ_AXES, EXCHANGE[name])  75 us
    pallas_call x36, Pallas kernels, __call__(): pl.pallas_call(run, out_shape=out_shape, in_specs=[pl.BlockSpec(memory_sp...  30.3 us
    ppermute x26, starting transfers between devices, by_tp(): return lax.ppermute(value, 'tp', [(k, k ^ flip) for k in range(TP)])  29.7 us
    ppermute x43, waiting for transfers between devices, by_seq(): return lax.ppermute(value, SEQ_AXES, EXCHANGE[name])  25.7 us
    unnamed x38, local copies, waits for them, and re-layouts  13.8 us
    ppermute x6, starting transfers between devices, shifted(): return lax.ppermute(value, SEQ_AXES, pairs)  13.3 us
    ppermute x6, waiting for transfers between devices, shifted(): return lax.ppermute(value, SEQ_AXES, pairs)  10.1 us
  transfers between devices with their start and end apart: 75, of which 31 were waited for; matrix products, arithmetic and copies ran while one was open for 0% of the time, Pallas kernels for 8%

profile of v2, /device:TPU:1, one launch (start us, length us, event | category | flops | bytes accessed | tf_op | source)
XLA Modules:
  0.0 310.0 jit_solution(15262526528174872563)
XLA Ops:
  6.0 5.8 %collective-permute-start.2 = (bf16[256,512]{1,0:T(8,128)(2,1)S(1)}, bf16[256,512]{1,0:T(8,128)(2,1)S(1)}, u32[]{:S(2)}, u32[]{:S(2)}) collective-permute-start(bf16[256,512]{1,0:T(8,128)(2,1)S(1)} %get-tuple-element.114.refs_1_.refs_3_.refs_0_), channel_id=1, source_target_pairs={{0,32},{8,40},{16,48},{24,56},{32,64},{40,72},{48,80},{56,88},{64,... | collective-permute-start | bytes 786440 | tf_op jit(solution)/shard_map/ppermute | solution.py:58
  31.7 5.7 %collective-permute-done.5.refs_1_ = bf16[64,2048]{1,0:T(8,128)(2,1)S(1)} collective-permute-done((bf16[64,2048]{1,0:T(8,128)(2,1)S(1)}, bf16[64,2048]{1,0:T(8,128)(2,1)S(1)}, u32[]{:S(2)}, u32[]{:S(2)}) %collective-permute-start.5) | collective-permute-done | bytes 262176 | tf_op jit(solution)/shard_map/ppermute | solution.py:53
  37.3 6.0 %collective-permute-done.6.refs_2_ = bf16[64,2048]{1,0:T(8,128)(2,1)S(1)} collective-permute-done((bf16[64,2048]{1,0:T(8,128)(2,1)S(1)}, bf16[64,2048]{1,0:T(8,128)(2,1)S(1)}, u32[]{:S(2)}, u32[]{:S(2)}) %collective-permute-start.6) | collective-permute-done | bytes 262176 | tf_op jit(solution)/shard_map/ppermute | solution.py:53
  51.5 3.9 %collective-permute-start.17 = (bf16[64,2048]{1,0:T(8,128)(2,1)S(1)}, bf16[64,2048]{1,0:T(8,128)(2,1)S(1)}, u32[]{:S(2)}, u32[]{:S(2)}) collective-permute-start(bf16[64,2048]{1,0:T(8,128)(2,1)S(1)} %pair_kernel.2.refs_0_), channel_id=1, source_target_pairs={{0,6},{1,7},{2,4},{3,5},{4,2},{5,3},{6,0},{7,1},{8,14},{9,15},{10,... | collective-permute-start | bytes 786440 | tf_op jit(solution)/shard_map/ppermute | solution.py:53
  63.1 4.1 %collective-permute-done.9.refs_8_.refs_2_ = bf16[256,640]{1,0:T(8,128)(2,1)S(1)} collective-permute-done((bf16[256,640]{1,0:T(8,128)(2,1)S(1)}, bf16[256,640]{1,0:T(8,128)(2,1)S(1)}, u32[]{:S(2)}, u32[]{:S(2)}) %collective-permute-start.9) | collective-permute-done | bytes 327712 | tf_op jit(solution)/shard_map/ppermute | solution.py:58
  70.9 4.2 %collective-permute-start.15 = (bf16[64,2048]{1,0:T(8,128)(2,1)S(1)}, bf16[64,2048]{1,0:T(8,128)(2,1)S(1)}, u32[]{:S(2)}, u32[]{:S(2)}) collective-permute-start(bf16[64,2048]{1,0:T(8,128)(2,1)S(1)} %pair_kernel.2.refs_0_), channel_id=1, source_target_pairs={{0,4},{1,5},{2,6},{3,7},{4,0},{5,1},{6,2},{7,3},{8,12},{9,13},{10,... | collective-permute-start | bytes 786440 | tf_op jit(solution)/shard_map/ppermute | solution.py:53
  77.9 9.1 %collective-permute-done.15.refs_1_ = bf16[64,2048]{1,0:T(8,128)(2,1)S(1)} collective-permute-done((bf16[64,2048]{1,0:T(8,128)(2,1)S(1)}, bf16[64,2048]{1,0:T(8,128)(2,1)S(1)}, u32[]{:S(2)}, u32[]{:S(2)}) %collective-permute-start.15) | collective-permute-done | bytes 262176 | tf_op jit(solution)/shard_map/ppermute | solution.py:53
  87.1 5.1 %ffn_kernel.1 = (bf16[256,2048]{1,0:T(8,128)(2,1)S(1)}, bf16[256,688]{1,0:T(8,128)(2,1)S(1)}, bf16[256,688]{1,0:T(8,128)(2,1)S(1)}, bf16[256,688]{1,0:T(8,128)(2...) custom-call(bf16[64,2048]{1,0:T(8,128)(2,1)S(1)} %pair_kernel.2.refs, ...), custom_call_target="tpu_custom_call" | custom-call | tf_op jit(solution)/shard_map/ffn_kernel/pallas_call | solution.py:114
  94.7 6.7 %collective-permute-done.22.refs_5_ = bf16[432,1024]{1,0:T(8,128)(2,1)S(1)} collective-permute-done((bf16[432,1024]{1,0:T(8,128)(2,1)S(1)}, bf16[432,1024]{1,0:T(8,128)(2,1)S(1)}, u32[]{:S(2)}, u32[]{:S(2)}) %collective-permute-start.22) | collective-permute-done | bytes 884768 | tf_op jit(solution)/shard_map/ppermute | solution.py:49
  104.7 5.0 %collective-permute-start.29 = (bf16[816,512]{1,0:T(8,128)(2,1)S(1)}, bf16[816,512]{1,0:T(8,128)(2,1)S(1)}, u32[]{:S(2)}, u32[]{:S(2)}) collective-permute-start(bf16[816,512]{1,0:T(8,128)(2,1)S(1)} %get-tuple-element.141), channel_id=1, source_target_pairs={{0,48},{8,56},{16,32},{24,40},{32,16},{40,24},{48,0},{56,8},{64,11... | collective-permute-start | bytes 2506760 | tf_op jit(solution)/shard_map/ppermute | solution.py:49
  112.9 5.5 %collective-permute-done.18.refs_1_ = bf16[64,2048]{1,0:T(8,128)(2,1)S(1)} collective-permute-done((bf16[64,2048]{1,0:T(8,128)(2,1)S(1)}, bf16[64,2048]{1,0:T(8,128)(2,1)S(1)}, u32[]{:S(2)}, u32[]{:S(2)}) %collective-permute-start.18) | collective-permute-done | bytes 262176 | tf_op jit(solution)/shard_map/ppermute | solution.py:53
  120.7 4.4 %collective-permute-done.20.refs_3_ = bf16[64,2048]{1,0:T(8,128)(2,1)S(1)} collective-permute-done((bf16[64,2048]{1,0:T(8,128)(2,1)S(1)}, bf16[64,2048]{1,0:T(8,128)(2,1)S(1)}, u32[]{:S(2)}, u32[]{:S(2)}) %collective-permute-start.20) | collective-permute-done | bytes 262176 | tf_op jit(solution)/shard_map/ppermute | solution.py:53
  125.3 5.6 %collective-permute-done.23.refs_1_ = bf16[32,2048]{1,0:T(8,128)(2,1)S(1)} collective-permute-done((bf16[32,2048]{1,0:T(8,128)(2,1)S(1)}, bf16[32,2048]{1,0:T(8,128)(2,1)S(1)}, u32[]{:S(2)}, u32[]{:S(2)}) %collective-permute-start.23) | collective-permute-done | bytes 131104 | tf_op jit(solution)/shard_map/ppermute | solution.py:53
  143.8 5.3 %collective-permute-done.25.refs_1_ = bf16[64,2048]{1,0:T(8,128)(2,1)S(1)} collective-permute-done((bf16[64,2048]{1,0:T(8,128)(2,1)S(1)}, bf16[64,2048]{1,0:T(8,128)(2,1)S(1)}, u32[]{:S(2)}, u32[]{:S(2)}) %collective-permute-start.25) | collective-permute-done | bytes 262176 | tf_op jit(solution)/shard_map/ppermute | solution.py:53
  152.2 5.9 %collective-permute-start.37 = (bf16[256,256]{1,0:T(8,128)(2,1)S(1)}, bf16[256,256]{1,0:T(8,128)(2,1)S(1)}, u32[]{:S(2)}, u32[]{:S(2)}) collective-permute-start(bf16[256,256]{1,0:T(8,128)(2,1)S(1)} %get-tuple-element.144.refs_2_.refs_7_), channel_id=1, source_target_pairs={{0,8},{8,0},{16,24},{24,16},{32,40},{40,32},{48,56},{56,48},{64,72... | collective-permute-start | bytes 393224 | tf_op jit(solution)/shard_map/ppermute | solution.py:49
  161.4 7.8 %collective-permute-start.39 = (bf16[816,128]{1,0:T(8,128)(2,1)S(1)}, bf16[816,128]{1,0:T(8,128)(2,1)S(1)}, u32[]{:S(2)}, u32[]{:S(2)}) collective-permute-start(bf16[816,128]{1,0:T(8,128)(2,1)S(1)} %get-tuple-element.156), channel_id=1, source_target_pairs={{0,64},{8,72},{16,80},{24,88},{32,96},{40,104},{48,112},{56,120},{... | collective-permute-start | bytes 626696 | tf_op jit(solution)/shard_map/ppermute | solution.py:49
  171.6 4.8 %collective-permute-done.41.refs_22_.refs_5_ = bf16[432,128]{1,0:T(8,128)(2,1)S(1)} collective-permute-done((bf16[432,128]{1,0:T(8,128)(2,1)S(1)}, bf16[432,128]{1,0:T(8,128)(2,1)S(1)}, u32[]{:S(2)}, u32[]{:S(2)}) %collective-permute-start.41) | collective-permute-done | bytes 110624 | tf_op jit(solution)/shard_map/ppermute | solution.py:49
  190.0 10.4 %collective-permute-done.42.refs_1_ = bf16[128,2048]{1,0:T(8,128)(2,1)S(1)} collective-permute-done((bf16[128,2048]{1,0:T(8,128)(2,1)S(1)}, bf16[128,2048]{1,0:T(8,128)(2,1)S(1)}, u32[]{:S(2)}, u32[]{:S(2)}) %collective-permute-start.42) | collective-permute-done | bytes 524320 | tf_op jit(solution)/shard_map/ppermute | solution.py:53
  209.0 4.3 %collective-permute-done.45.refs_1_ = bf16[64,2048]{1,0:T(8,128)(2,1)S(1)} collective-permute-done((bf16[64,2048]{1,0:T(8,128)(2,1)S(1)}, bf16[64,2048]{1,0:T(8,128)(2,1)S(1)}, u32[]{:S(2)}, u32[]{:S(2)}) %collective-permute-start.45) | collective-permute-done | bytes 262176 | tf_op jit(solution)/shard_map/ppermute | solution.py:53
  213.8 9.2 %collective-permute-done.50.refs_1_ = bf16[32,4224]{1,0:T(8,128)(2,1)S(1)} collective-permute-done((bf16[32,4224]{1,0:T(8,128)(2,1)S(1)}, bf16[32,4224]{1,0:T(8,128)(2,1)S(1)}, u32[]{:S(2)}, u32[]{:S(2)}) %collective-permute-start.50) | collective-permute-done | bytes 270368 | tf_op jit(solution)/shard_map/ppermute | solution.py:53
  228.5 15.3 %collective-permute-done.51.refs_1_ = bf16[32,4096]{1,0:T(8,128)(2,1)S(1)} collective-permute-done((bf16[32,4096]{1,0:T(8,128)(2,1)S(1)}, bf16[32,4096]{1,0:T(8,128)(2,1)S(1)}, u32[]{:S(2)}, u32[]{:S(2)}) %collective-permute-start.51) | collective-permute-done | bytes 262176 | tf_op jit(solution)/shard_map/ppermute | solution.py:53
  244.5 4.9 %collective-permute-done.55.refs_1_ = bf16[64,2048]{1,0:T(8,128)(2,1)S(1)} collective-permute-done((bf16[64,2048]{1,0:T(8,128)(2,1)S(1)}, bf16[64,2048]{1,0:T(8,128)(2,1)S(1)}, u32[]{:S(2)}, u32[]{:S(2)}) %collective-permute-start.55) | collective-permute-done | bytes 262176 | tf_op jit(solution)/shard_map/ppermute | solution.py:53
  250.9 5.4 %collective-permute-start.71 = (bf16[2064,1024]{1,0:T(8,128)(2,1)S(1)}, bf16[2064,1024]{1,0:T(8,128)(2,1)S(1)}, u32[]{:S(2)}, u32[]{:S(2)}) collective-permute-start(bf16[2064,1024]{1,0:T(8,128)(2,1)S(1)} %ffn_halves_kernel.1.refs_6_.own_ref), channel_id=1, source_target_pairs={{0,8},{8,0},{16,24},{24,16},{32,40},{40,32},{48,56},{56,48},{64,72... | collective-permute-start | bytes 12681224 | tf_op jit(solution)/shard_map/ppermute | solution.py:49
  298.5 3.8 %collective-permute-start.72 = (bf16[1024,384]{1,0:T(8,128)(2,1)S(1)}, bf16[1024,384]{1,0:T(8,128)(2,1)S(1)}, u32[]{:S(2)}, u32[]{:S(2)}) collective-permute-start(bf16[1024,384]{1,0:T(8,128)(2,1)S(1)} %get-tuple-element.208.refs_0_), channel_id=1, source_target_pairs={{0,8},{8,0},{16,24},{24,16},{32,40},{40,32},{48,56},{56,48},{64,72... | collective-permute-start | bytes 2359304 | tf_op jit(solution)/shard_map/ppermute | solution.py:49
  (206 shorter events, 160.1 us)
Async XLA Ops:
  50.2 17.1 %collective-permute-start.9 = (bf16[256,640]{1,0:T(8,128)(2,1)S(1)}, bf16[256,640]{1,0:T(8,128)(2,1)S(1)}, u32[]{:S(2)}, u32[]{:S(2)}) collective-permute-start(bf16[256,640]{1,0:T(8,128)(2,1)S(1)} %shard_map.194.refs_0_.refs_1_), channel_id=1, source_target_pairs={{16,0},{24,8},{32,16},{40,24},{48,32},{56,40},{64,48},{72,56},{80,... | collective-permute-start | bytes 983048 | tf_op jit(solution)/shard_map/ppermute | solution.py:58
  51.5 19.4 %collective-permute-start.17 = (bf16[64,2048]{1,0:T(8,128)(2,1)S(1)}, bf16[64,2048]{1,0:T(8,128)(2,1)S(1)}, u32[]{:S(2)}, u32[]{:S(2)}) collective-permute-start(bf16[64,2048]{1,0:T(8,128)(2,1)S(1)} %pair_kernel.2.refs_0_), channel_id=1, source_target_pairs={{0,6},{1,7},{2,4},{3,5},{4,2},{5,3},{6,0},{7,1},{8,14},{9,15},{10,... | collective-permute-start | bytes 786440 | tf_op jit(solution)/shard_map/ppermute | solution.py:53
  55.4 37.2 %collective-permute-start.12 = (bf16[256,640]{1,0:T(8,128)(2,1)S(1)}, bf16[256,640]{1,0:T(8,128)(2,1)S(1)}, u32[]{:S(2)}, u32[]{:S(2)}) collective-permute-start(bf16[256,640]{1,0:T(8,128)(2,1)S(1)} %shard_map.194.refs_0_.refs_1_), channel_id=1, source_target_pairs={{0,8},{8,0},{16,24},{24,16},{32,40},{40,32},{48,56},{56,48},{64,72... | collective-permute-start | bytes 983048 | tf_op jit(solution)/shard_map/ppermute | solution.py:49
  59.8 32.8 %collective-permute-start.13 = (bf16[256,640]{1,0:T(8,128)(2,1)S(1)}, bf16[256,640]{1,0:T(8,128)(2,1)S(1)}, u32[]{:S(2)}, u32[]{:S(2)}) collective-permute-start(bf16[256,640]{1,0:T(8,128)(2,1)S(1)} %collective-permute-done.11.refs_9_.refs_4_), channel_id=1, source_target_pairs={{0,8},{8,0},{16,24},{24,16},{32,40},{40,32},{48,56},{56,48},{64,72... | collective-permute-start | bytes 983048 | tf_op jit(solution)/shard_map/ppermute | solution.py:49
  67.2 25.4 %collective-permute-start.10 = (bf16[256,640]{1,0:T(8,128)(2,1)S(1)}, bf16[256,640]{1,0:T(8,128)(2,1)S(1)}, u32[]{:S(2)}, u32[]{:S(2)}) collective-permute-start(bf16[256,640]{1,0:T(8,128)(2,1)S(1)} %collective-permute-done.9.refs_8_.refs_2_), channel_id=1, source_target_pairs={{0,8},{8,0},{16,24},{24,16},{32,40},{40,32},{48,56},{56,48},{64,72... | collective-permute-start | bytes 983048 | tf_op jit(solution)/shard_map/ppermute | solution.py:49
  70.9 16.1 %collective-permute-start.15 = (bf16[64,2048]{1,0:T(8,128)(2,1)S(1)}, bf16[64,2048]{1,0:T(8,128)(2,1)S(1)}, u32[]{:S(2)}, u32[]{:S(2)}) collective-permute-start(bf16[64,2048]{1,0:T(8,128)(2,1)S(1)} %pair_kernel.2.refs_0_), channel_id=1, source_target_pairs={{0,4},{1,5},{2,6},{3,7},{4,0},{5,1},{6,2},{7,3},{8,12},{9,13},{10,... | collective-permute-start | bytes 786440 | tf_op jit(solution)/shard_map/ppermute | solution.py:53
  103.0 32.1 %collective-permute-start.28 = (bf16[816,512]{1,0:T(8,128)(2,1)S(1)}, bf16[816,512]{1,0:T(8,128)(2,1)S(1)}, u32[]{:S(2)}, u32[]{:S(2)}) collective-permute-start(bf16[816,512]{1,0:T(8,128)(2,1)S(1)} %get-tuple-element.139), channel_id=1, source_target_pairs={{0,16},{8,24},{16,0},{24,8},{32,48},{40,56},{48,32},{56,40},{64,80... | collective-permute-start | bytes 2506760 | tf_op jit(solution)/shard_map/ppermute | solution.py:49
  104.7 30.4 %collective-permute-start.29 = (bf16[816,512]{1,0:T(8,128)(2,1)S(1)}, bf16[816,512]{1,0:T(8,128)(2,1)S(1)}, u32[]{:S(2)}, u32[]{:S(2)}) collective-permute-start(bf16[816,512]{1,0:T(8,128)(2,1)S(1)} %get-tuple-element.141), channel_id=1, source_target_pairs={{0,48},{8,56},{16,32},{24,40},{32,16},{40,24},{48,0},{56,8},{64,11... | collective-permute-start | bytes 2506760 | tf_op jit(solution)/shard_map/ppermute | solution.py:49
  109.7 15.3 %collective-permute-start.20 = (bf16[64,2048]{1,0:T(8,128)(2,1)S(1)}, bf16[64,2048]{1,0:T(8,128)(2,1)S(1)}, u32[]{:S(2)}, u32[]{:S(2)}) collective-permute-start(bf16[64,2048]{1,0:T(8,128)(2,1)S(1)} %get-tuple-element.128), channel_id=1, source_target_pairs={{0,6},{1,7},{2,4},{3,5},{4,2},{5,3},{6,0},{7,1},{8,14},{9,15},{10,... | collective-permute-start | bytes 786440 | tf_op jit(solution)/shard_map/ppermute | solution.py:53
  118.4 16.7 %collective-permute-start.30 = (bf16[432,512]{1,0:T(8,128)(2,1)S(1)}, bf16[432,512]{1,0:T(8,128)(2,1)S(1)}, u32[]{:S(2)}, u32[]{:S(2)}) collective-permute-start(bf16[432,512]{1,0:T(8,128)(2,1)S(1)} %get-tuple-element.142), channel_id=1, source_target_pairs={{0,64},{8,72},{16,80},{24,88},{32,96},{40,104},{48,112},{56,120},{... | collective-permute-start | bytes 1327112 | tf_op jit(solution)/shard_map/ppermute | solution.py:49
  135.7 25.5 %collective-permute-start.33 = (bf16[816,256]{1,0:T(8,128)(2,1)S(1)}, bf16[816,256]{1,0:T(8,128)(2,1)S(1)}, u32[]{:S(2)}, u32[]{:S(2)}) collective-permute-start(bf16[816,256]{1,0:T(8,128)(2,1)S(1)} %get-tuple-element.145), channel_id=1, source_target_pairs={{0,48},{8,56},{16,32},{24,40},{32,16},{40,24},{48,0},{56,8},{64,11... | collective-permute-start | bytes 1253384 | tf_op jit(solution)/shard_map/ppermute | solution.py:49
  135.8 25.3 %collective-permute-start.34 = (bf16[816,256]{1,0:T(8,128)(2,1)S(1)}, bf16[816,256]{1,0:T(8,128)(2,1)S(1)}, u32[]{:S(2)}, u32[]{:S(2)}) collective-permute-start(bf16[816,256]{1,0:T(8,128)(2,1)S(1)} %get-tuple-element.147), channel_id=1, source_target_pairs={{0,64},{8,72},{16,80},{24,88},{32,96},{40,104},{48,112},{56,120},{... | collective-permute-start | bytes 1253384 | tf_op jit(solution)/shard_map/ppermute | solution.py:49
  149.6 20.7 %collective-permute-start.32 = (bf16[256,256]{1,0:T(8,128)(2,1)S(1)}, bf16[256,256]{1,0:T(8,128)(2,1)S(1)}, u32[]{:S(2)}, u32[]{:S(2)}) collective-permute-start(bf16[256,256]{1,0:T(8,128)(2,1)S(1)} %get-tuple-element.144.refs_2_.refs_7_), channel_id=1, source_target_pairs={{32,0},{40,8},{48,16},{56,24},{64,32},{72,40},{80,48},{88,56},{96,... | collective-permute-start | bytes 393224 | tf_op jit(solution)/shard_map/ppermute | solution.py:58
  150.9 19.4 %collective-permute-start.31 = (bf16[256,256]{1,0:T(8,128)(2,1)S(1)}, bf16[256,256]{1,0:T(8,128)(2,1)S(1)}, u32[]{:S(2)}, u32[]{:S(2)}) collective-permute-start(bf16[256,256]{1,0:T(8,128)(2,1)S(1)} %get-tuple-element.144.refs_2_.refs_7_), channel_id=1, source_target_pairs={{16,0},{24,8},{32,16},{40,24},{48,32},{56,40},{64,48},{72,56},{80,... | collective-permute-start | bytes 393224 | tf_op jit(solution)/shard_map/ppermute | solution.py:58
  152.2 18.7 %collective-permute-start.37 = (bf16[256,256]{1,0:T(8,128)(2,1)S(1)}, bf16[256,256]{1,0:T(8,128)(2,1)S(1)}, u32[]{:S(2)}, u32[]{:S(2)}) collective-permute-start(bf16[256,256]{1,0:T(8,128)(2,1)S(1)} %get-tuple-element.144.refs_2_.refs_7_), channel_id=1, source_target_pairs={{0,8},{8,0},{16,24},{24,16},{32,40},{40,32},{48,56},{56,48},{64,72... | collective-permute-start | bytes 393224 | tf_op jit(solution)/shard_map/ppermute | solution.py:49
  203.1 20.3 %collective-permute-start.53 = (bf16[1200,256]{1,0:T(8,128)(2,1)S(1)}, bf16[1200,256]{1,0:T(8,128)(2,1)S(1)}, u32[]{:S(2)}, u32[]{:S(2)}) collective-permute-start(bf16[1200,256]{1,0:T(8,128)(2,1)S(1)} %get-tuple-element.181.refs_1_), channel_id=1, source_target_pairs={{0,48},{8,56},{16,32},{24,40},{32,16},{40,24},{48,0},{56,8},{64,11... | collective-permute-start | bytes 1843208 | tf_op jit(solution)/shard_map/ppermute | solution.py:49
  203.8 19.6 %collective-permute-start.54 = (bf16[1200,256]{1,0:T(8,128)(2,1)S(1)}, bf16[1200,256]{1,0:T(8,128)(2,1)S(1)}, u32[]{:S(2)}, u32[]{:S(2)}) collective-permute-start(bf16[1200,256]{1,0:T(8,128)(2,1)S(1)} %get-tuple-element.182.refs_2_), channel_id=1, source_target_pairs={{0,64},{8,72},{16,80},{24,88},{32,96},{40,104},{48,112},{56,120},{... | collective-permute-start | bytes 1843208 | tf_op jit(solution)/shard_map/ppermute | solution.py:49
  223.7 26.8 %collective-permute-start.60 = (bf16[944,512]{1,0:T(8,128)(2,1)S(1)}, bf16[944,512]{1,0:T(8,128)(2,1)S(1)}, u32[]{:S(2)}, u32[]{:S(2)}) collective-permute-start(bf16[944,512]{1,0:T(8,128)(2,1)S(1)} %get-tuple-element.191.refs_1_), channel_id=1, source_target_pairs={{0,48},{8,56},{16,32},{24,40},{32,16},{40,24},{48,0},{56,8},{64,11... | collective-permute-start | bytes 2899976 | tf_op jit(solution)/shard_map/ppermute | solution.py:49
  226.3 24.2 %collective-permute-start.59 = (bf16[944,512]{1,0:T(8,128)(2,1)S(1)}, bf16[944,512]{1,0:T(8,128)(2,1)S(1)}, u32[]{:S(2)}, u32[]{:S(2)}) collective-permute-start(bf16[944,512]{1,0:T(8,128)(2,1)S(1)} %get-tuple-element.186.refs_2_.refs_0_), channel_id=1, source_target_pairs={{0,16},{8,24},{16,0},{24,8},{32,48},{40,56},{48,32},{56,40},{64,80... | collective-permute-start | bytes 2899976 | tf_op jit(solution)/shard_map/ppermute | solution.py:49
  226.4 24.2 %collective-permute-start.61 = (bf16[560,512]{1,0:T(8,128)(2,1)S(1)}, bf16[560,512]{1,0:T(8,128)(2,1)S(1)}, u32[]{:S(2)}, u32[]{:S(2)}) collective-permute-start(bf16[560,512]{1,0:T(8,128)(2,1)S(1)} %get-tuple-element.192.refs_2_), channel_id=1, source_target_pairs={{0,64},{8,72},{16,80},{24,88},{32,96},{40,104},{48,112},{56,120},{... | collective-permute-start | bytes 1720328 | tf_op jit(solution)/shard_map/ppermute | solution.py:49
  250.9 29.9 %collective-permute-start.71 = (bf16[2064,1024]{1,0:T(8,128)(2,1)S(1)}, bf16[2064,1024]{1,0:T(8,128)(2,1)S(1)}, u32[]{:S(2)}, u32[]{:S(2)}) collective-permute-start(bf16[2064,1024]{1,0:T(8,128)(2,1)S(1)} %ffn_halves_kernel.1.refs_6_.own_ref), channel_id=1, source_target_pairs={{0,8},{8,0},{16,24},{24,16},{32,40},{40,32},{48,56},{56,48},{64,72... | collective-permute-start | bytes 12681224 | tf_op jit(solution)/shard_map/ppermute | solution.py:49
  256.4 16.3 %collective-permute-start.58 = (bf16[128,2048]{1,0:T(8,128)(2,1)S(1)}, bf16[128,2048]{1,0:T(8,128)(2,1)S(1)}, u32[]{:S(2)}, u32[]{:S(2)}) collective-permute-start(bf16[128,2048]{1,0:T(8,128)(2,1)S(1)} %get-tuple-element.190.refs_2_), channel_id=1, source_target_pairs={{0,2},{1,3},{2,0},{3,1},{4,6},{5,7},{6,4},{7,5},{8,10},{9,11},{10,... | collective-permute-start | bytes 1572872 | tf_op jit(solution)/shard_map/ppermute | solution.py:53
  256.8 15.9 %collective-permute-start.57 = (bf16[128,2048]{1,0:T(8,128)(2,1)S(1)}, bf16[128,2048]{1,0:T(8,128)(2,1)S(1)}, u32[]{:S(2)}, u32[]{:S(2)}) collective-permute-start(bf16[128,2048]{1,0:T(8,128)(2,1)S(1)} %get-tuple-element.189.refs_7_.refs_0_), channel_id=1, source_target_pairs={{0,6},{1,7},{2,4},{3,5},{4,2},{5,3},{6,0},{7,1},{8,14},{9,15},{10,... | collective-permute-start | bytes 1572872 | tf_op jit(solution)/shard_map/ppermute | solution.py:53
  278.5 17.1 %collective-permute-start.69 = (bf16[512,384]{1,0:T(8,128)(2,1)S(1)}, bf16[512,384]{1,0:T(8,128)(2,1)S(1)}, u32[]{:S(2)}, u32[]{:S(2)}) collective-permute-start(bf16[512,384]{1,0:T(8,128)(2,1)S(1)} %get-tuple-element.206.refs_2_), channel_id=1, source_target_pairs={{0,48},{8,56},{16,32},{24,40},{32,16},{40,24},{48,0},{56,8},{64,11... | collective-permute-start | bytes 1179656 | tf_op jit(solution)/shard_map/ppermute | solution.py:49
  (70 other events, 857.0 us)
